TPU v7x, 256 devices: a whole 4x4x8 slice. The times are simulated.
256 devices in a mesh: seq: 8 (over z_hi, x), roll: 32 (over y, z_lo, core).
Axes of the slice: x: 4, y: 4, z: 8 (z_hi: 2, z_lo: 4; z = z_hi * 4 + z_lo), core: 2. Of those that a mesh axis runs over, the one named last changes fastest.
Arguments:
- x_prompt: bfloat16 [2048, 4096], P('seq', 'roll'), may hold values from -6 to 6
- dt_prompt: float32 [64, 2048], P('roll', 'seq'), may hold values from 0.01 to 0.24, as said below
- b_prompt: bfloat16 [2048, 512], P('seq'), may hold values from -1.796875 to 1.796875
- x_roll: bfloat16 [32, 1024, 4096], P('roll', 'seq'), may hold values from -6 to 6
- dt_roll: float32 [32, 64, 1024], P('roll', None, 'seq'), may hold values from 0.01 to 0.24, as said below
- b_roll: bfloat16 [32, 1024, 512], P('roll', 'seq'), may hold values from -1.796875 to 1.796875
- c_roll: bfloat16 [32, 1024, 512], P('roll', 'seq'), may hold values from -1.796875 to 1.796875
- rate: float32 [64], replicated, may hold values from 0.002 to 1, as said below
- skip: float32 [64], replicated, may hold values from 0.1 to 1.9
- grad_y: bfloat16 [32, 1024, 4096], P('roll', 'seq'), may hold values from -6 to 6
- roll_len: int32 [32], P('roll'), may hold values from 256 to 1024
- prompt_len: int32 [1], replicated, may hold values from 1024 to 2048
Outputs:
- grad_x_prompt: bfloat16 [2048, 4096], P('seq', 'roll')
- grad_b_prompt: bfloat16 [2048, 512], P('seq')
- grad_dt_prompt: float32 [64, 2048], P('roll', 'seq')
- grad_x_roll: bfloat16 [32, 1024, 4096], P('roll', 'seq')
- grad_b_roll: bfloat16 [32, 1024, 512], P('roll', 'seq')
- grad_c_roll: bfloat16 [32, 1024, 512], P('roll', 'seq')
- grad_dt_roll: float32 [32, 64, 1024], P('roll', None, 'seq')
Inputs may be any that keep to these rules, and one draw needn't show every extreme that they name: `dt_prompt`: positive step sizes. `dt_roll`: positive step sizes. `rate`: positive rates.
All inputs are finite; a program needn't handle non-finite values.
Results may differ from a plain program's by a relative error of at most 0.012.
Values may be sent and summed in bfloat16 or wider, within the bound.
A program may use at most 128 MiB of HBM per device.

v0:
```python
import jax
import jax.numpy as jnp
from jax import lax
from jax.sharding import PartitionSpec as P

HEAD_DIM = 64
STATE = 128
GROUPS = 4


def prefix(value, axis, combine, identity, reverse):
    size, mine = (lax.axis_size(axis), lax.axis_index(axis))
    everything = jax.tree.map(lambda part: lax.all_gather(part, axis), value)
    start = jax.tree.map(
        lambda part, zero: jnp.broadcast_to(jnp.asarray(zero, part.dtype), part.shape),
        value,
        identity,
    )

    def lap(k, before):
        at = size - 1 - k if reverse else k
        reached = at > mine if reverse else at < mine
        new = combine(before, jax.tree.map(lambda part: part[at], everything))
        return jax.tree.map(lambda a, b: jnp.where(reached, a, b), new, before)

    return lax.fori_loop(0, size, lap, start)


def passed_along(value, axis, steps):
    count = lax.axis_size(axis)
    initial, last = (max(0, -steps), min(count, count - steps))
    return lax.ppermute(value, axis, [(source, source + steps) for source in range(initial, last)])


def exact_product(spec, *operands):
    return jnp.einsum(
        spec,
        *[operand.astype(jnp.float32) for operand in operands],
        precision=lax.Precision.HIGHEST
    )


def lead_groups(array_in, groups):
    return array_in.reshape((groups, array_in.shape[0] // groups) + array_in.shape[1:])


def token_groups(array_in, groups):
    return array_in.reshape(
        (array_in.shape[0], groups, array_in.shape[1] // groups) + array_in.shape[2:]
    )


def chain_link(earlier, following):
    return (earlier[0] * following[0], following[0][:, None, None] * earlier[1] + following[1])


def local_forward(inputs, b_rows, step_rows, log_decay):
    groups = b_rows.shape[1]
    cumulative = jnp.cumsum(log_decay, axis=1)
    weights = jnp.exp(cumulative[:, -1:] - cumulative) * step_rows
    state = exact_product(
        "gkt,tgkp,tgn->gkpn", lead_groups(weights, groups), token_groups(inputs, groups), b_rows
    )
    return (
        jnp.exp(cumulative[:, -1]),
        state.reshape(log_decay.shape[0], inputs.shape[2], b_rows.shape[2]),
    )


def grad_summary(cotangent, c_rows, log_decay):
    groups = c_rows.shape[1]
    rising = jnp.exp(jnp.cumsum(log_decay, axis=1))
    summary = exact_product(
        "gkt,tgkp,tgn->gkpn", lead_groups(rising, groups), token_groups(cotangent, groups), c_rows
    )
    return summary.reshape(log_decay.shape[0], cotangent.shape[2], c_rows.shape[2])


def block_terms(
    inputs,
    cotangent,
    b_rows,
    c_rows,
    step_rows,
    log_decay,
    rate,
    skip,
    live,
    entry_state,
    beyond_grad,
    summary,
):
    groups = b_rows.shape[1]
    length = inputs.shape[0]
    head_count = log_decay.shape[0]
    per_group = head_count // groups
    cumulative = jnp.cumsum(log_decay, axis=1)
    end_log = cumulative[:, -1:]
    causal_mask = jnp.arange(length)[:, None] >= jnp.arange(length)[None, :]
    gaps = cumulative[:, :, None] - cumulative[:, None, :]
    segment = jnp.where(causal_mask, jnp.exp(jnp.where(causal_mask, gaps, 0.0)), 0.0)
    intersection_cb = jnp.einsum("vgn,ugn->gvu", c_rows, b_rows, preferred_element_type=jnp.float32)
    intersection_gx = jnp.einsum(
        "vhp,uhp->hvu", cotangent, inputs, preferred_element_type=jnp.float32
    )
    weighted = segment * intersection_gx
    intersection_heads = jnp.repeat(intersection_cb, per_group, axis=0)
    paired = weighted * intersection_heads * step_rows[:, None, :]
    pooled = jnp.sum(
        (weighted * step_rows[:, None, :]).reshape(groups, per_group, length, length), axis=1
    )
    tail_decay = jnp.exp(end_log - cumulative)
    beyond_groups = lead_groups(beyond_grad, groups)
    pulled = exact_product("tgn,gkpn->tgkp", b_rows, beyond_groups).reshape(length, head_count, -1)
    slope = (
        exact_product("hvu,vhp->uhp", segment * intersection_heads, cotangent)
        + tail_decay.T[:, :, None] * pulled
    )
    inputs_wide = inputs.astype(jnp.float32)
    grad_inputs = step_rows.T[:, :, None] * slope + skip[None, :, None] * cotangent.astype(
        jnp.float32
    )
    outer_weight = (step_rows * tail_decay).T
    grad_b = exact_product("gvu,vgn->ugn", pooled, c_rows) + exact_product(
        "tgkp,gkpn->tgn",
        token_groups(inputs_wide * outer_weight[:, :, None], groups),
        beyond_groups,
    )
    seen = exact_product(
        "tgkp,gkpn->tgkn", token_groups(cotangent, groups), lead_groups(entry_state, groups)
    )
    rising = jnp.exp(cumulative).T
    grad_c = exact_product("gvu,ugn->vgn", pooled, b_rows) + jnp.sum(
        seen * token_groups(rising, groups)[..., None], axis=2
    )
    entry_terms = rising * jnp.sum(
        seen * c_rows[:, :, None, :].astype(jnp.float32), axis=3
    ).reshape(length, head_count)
    leave_terms = outer_weight * jnp.sum(inputs_wide * pulled, axis=2)
    carried = jnp.sum(leave_terms, axis=0) + jnp.exp(end_log[:, 0]) * jnp.sum(
        beyond_grad * entry_state, axis=(1, 2)
    )
    final_slot = (jnp.arange(length) == length - 1).astype(jnp.float32)
    slopes_log = (
        jnp.sum(paired, axis=2)
        - jnp.sum(paired, axis=1)
        + (entry_terms - leave_terms).T
        + carried[:, None] * final_slot[None, :]
    )
    grad_log = lax.cumsum(slopes_log, axis=1, reverse=True)
    grad_step = live[None, :] * (jnp.sum(inputs_wide * slope, axis=2).T - rate[:, None] * grad_log)
    backward_state = summary + jnp.exp(end_log)[:, :, None] * beyond_grad
    return (grad_inputs, grad_b, grad_c, grad_step, backward_state)


def prompt_terms(inputs, b_rows, step_rows, log_decay, rate, live, entry_state, beyond_grad):
    length = inputs.shape[0]
    head_count = log_decay.shape[0]
    cumulative = jnp.cumsum(log_decay, axis=1)
    end_log = cumulative[:, -1:]
    tail_decay = jnp.exp(end_log - cumulative)
    beyond_groups = lead_groups(beyond_grad, 1)
    pulled = exact_product("tgn,gkpn->tgkp", b_rows, beyond_groups).reshape(length, head_count, -1)
    slope = tail_decay.T[:, :, None] * pulled
    inputs_wide = inputs.astype(jnp.float32)
    grad_inputs = step_rows.T[:, :, None] * slope
    outer_weight = (step_rows * tail_decay).T
    grad_b = exact_product(
        "tgkp,gkpn->tgn", token_groups(inputs_wide * outer_weight[:, :, None], 1), beyond_groups
    )
    leave_terms = outer_weight * jnp.sum(inputs_wide * pulled, axis=2)
    carried = jnp.sum(leave_terms, axis=0) + jnp.exp(end_log[:, 0]) * jnp.sum(
        beyond_grad * entry_state, axis=(1, 2)
    )
    final_slot = (jnp.arange(length) == length - 1).astype(jnp.float32)
    slopes_log = -leave_terms.T + carried[:, None] * final_slot[None, :]
    grad_log = lax.cumsum(slopes_log, axis=1, reverse=True)
    grad_step = live[None, :] * (jnp.sum(inputs_wide * slope, axis=2).T - rate[:, None] * grad_log)
    return (grad_inputs, grad_b, grad_step)


def prompt_chain(decay, landed):
    quiet = (jnp.ones_like(decay), jnp.zeros_like(landed))
    _, scanned = prefix((decay, decay[:, None, None] * landed), "seq", chain_link, quiet, True)
    return scanned + landed


def local(
    x_prompt,
    dt_prompt,
    b_prompt,
    x_roll,
    dt_roll,
    b_roll,
    c_roll,
    rate,
    skip,
    grad_y,
    roll_len,
    prompt_len,
):
    seq_count = lax.axis_size("seq")
    seq_place = lax.axis_index("seq")
    roll_place = lax.axis_index("roll")
    head_count = rate.shape[0]
    prompt_heads = dt_prompt.shape[0]
    prompt_rows = x_prompt.shape[0]
    rollout_rows = x_roll.shape[1]
    first_row = (seq_place == 0).astype(jnp.float32)
    last_row = (seq_place == seq_count - 1).astype(jnp.float32)
    positions_p = seq_place * prompt_rows + jnp.arange(prompt_rows)
    live_p = (positions_p >= prompt_rows * seq_count - prompt_len[0]).astype(jnp.float32)
    rate_p = lax.dynamic_slice_in_dim(rate, roll_place * prompt_heads, prompt_heads)
    step_p = dt_prompt * live_p[None, :]
    logd_p = -rate_p[:, None] * step_p
    inputs_p = x_prompt.reshape(prompt_rows, prompt_heads, HEAD_DIM)
    group_id = roll_place * prompt_heads // (head_count // GROUPS)
    b_rows_p = lax.dynamic_slice_in_dim(b_prompt, group_id * STATE, STATE, 1).reshape(
        prompt_rows, 1, STATE
    )
    decay_p, local_p = local_forward(inputs_p, b_rows_p, step_p, logd_p)
    quiet_p = (jnp.ones_like(decay_p), jnp.zeros_like(local_p))
    _, enter_p = prefix((decay_p, local_p), "seq", chain_link, quiet_p, False)
    prompt_tail = decay_p[:, None, None] * enter_p + local_p
    assembled = lax.all_gather(prompt_tail, "roll", axis=0, tiled=True)
    fork = passed_along(assembled, "seq", 1 - seq_count)
    fork = fork * first_row
    inputs_r = x_roll[0].reshape(rollout_rows, head_count, HEAD_DIM)
    b_rows_r = b_roll[0].reshape(rollout_rows, GROUPS, STATE)
    c_rows_r = c_roll[0].reshape(rollout_rows, GROUPS, STATE)
    live_mask = seq_place * rollout_rows + jnp.arange(rollout_rows) < roll_len[0]
    live_r = live_mask.astype(jnp.float32)
    cotangent = jnp.where(
        live_mask[:, None, None],
        grad_y[0].reshape(rollout_rows, head_count, HEAD_DIM),
        jnp.zeros((), jnp.bfloat16),
    )
    step_r = dt_roll[0] * live_r[None, :]
    logd_r = -rate[:, None] * step_r
    decay_r, local_r = local_forward(inputs_r, b_rows_r, step_r, logd_r)
    quiet_r = (jnp.ones_like(decay_r), jnp.zeros_like(local_r))
    _, scanned_r = prefix(
        (decay_r, local_r + decay_r[:, None, None] * fork), "seq", chain_link, quiet_r, False
    )
    enter_r = scanned_r + fork
    summary_r = grad_summary(cotangent, c_rows_r, logd_r)
    _, beyond_r = prefix((decay_r, summary_r), "seq", chain_link, quiet_r, True)
    grad_inputs_r, grad_b_r, grad_c_r, grad_step_r, back_r = block_terms(
        inputs_r,
        cotangent,
        b_rows_r,
        c_rows_r,
        step_r,
        logd_r,
        rate,
        skip,
        live_r,
        enter_r,
        beyond_r,
        summary_r,
    )
    outgoing = back_r * first_row
    grad_x_out = grad_inputs_r.reshape(1, rollout_rows, head_count * HEAD_DIM).astype(jnp.bfloat16)
    grad_b_out = grad_b_r.reshape(1, rollout_rows, GROUPS * STATE).astype(jnp.bfloat16)
    grad_c_out = grad_c_r.reshape(1, rollout_rows, GROUPS * STATE).astype(jnp.bfloat16)
    grad_dt_out = grad_step_r[None]
    moved_grad = passed_along(outgoing, "seq", seq_count - 1)
    landed = lax.psum_scatter(moved_grad, "roll", scatter_dimension=0, tiled=True)
    beyond_p = prompt_chain(decay_p, landed * last_row)
    grad_inputs_p, grad_b_part, grad_step_p = prompt_terms(
        inputs_p, b_rows_p, step_p, logd_p, rate_p, live_p, enter_p, beyond_p
    )
    selector = (jnp.arange(GROUPS) == group_id).astype(jnp.float32)
    placed = grad_b_part * selector[None, :, None]
    grad_b_whole = lax.psum(placed, "roll")
    return (
        grad_inputs_p.reshape(prompt_rows, prompt_heads * HEAD_DIM).astype(jnp.bfloat16),
        grad_b_whole.reshape(prompt_rows, GROUPS * STATE).astype(jnp.bfloat16),
        grad_step_p,
        grad_x_out,
        grad_b_out,
        grad_c_out,
        grad_dt_out,
    )


def solution(mesh):
    in_specs = (
        P("seq", "roll"),
        P("roll", "seq"),
        P("seq", None),
        P("roll", "seq", None),
        P("roll", None, "seq"),
        P("roll", "seq", None),
        P("roll", "seq", None),
        P(),
        P(),
        P("roll", "seq", None),
        P("roll"),
        P(),
    )
    out_specs = (
        P("seq", "roll"),
        P("seq", None),
        P("roll", "seq"),
        P("roll", "seq", None),
        P("roll", "seq", None),
        P("roll", "seq", None),
        P("roll", None, "seq"),
    )
    return jax.shard_map(local, mesh=mesh, in_specs=in_specs, out_specs=out_specs, check_vma=False)
```

profile of v0, /device:TPU:1, one launch (start us, length us, event | category | flops | bytes accessed | tf_op | source)
XLA Modules:
  0.0 1242.5 jit_solution(14553881757426343547)
XLA Ops:
  20.9 32.7 %all-reduce.2 = (f32[16]{0:T(128)}, f32[512]{0:T(512)S(1)}) all-reduce(f32[16]{0:T(128)S(1)} %get-tuple-element.630, f32[512]{0:T(512)S(1)} %dynamic-update-slice.1), channel_id=2, replica_groups=mesh['seq'=8,'roll'=32] {'seq'}, use_global_device_ids=true, to_apply=%add | all-reduce | flops 528 | bytes 4224
  53.7 272.7 %all-gather.9.cloned.1.call-done = f32[8,64,64,128]{3,2,1,0:T(8,128)} async-done(((f32[1,64,64,128]{3,2,1,0:T(8,128)}), f32[8,64,64,128]{3,2,1,0:T(8,128)}) %all-gather.9.cloned.1.call-update) | async-done | bytes 16777232 | tf_op jit(solution)/shard_map/all_gather | solution.py:13
  326.4 17.1 %while.60 = (s32[]{:T(128)}, f32[64,64,128]{2,1,0:T(8,128)S(1)}, s32[]{:T(128)}, f32[8,64]{1,0:T(8,128)S(1)}, f32[8,64,64,128]{3,2,1,0:T(8,128)}, /*index=5*/s32[]{:T(128)}, s32[]{:T(128)}, s32[]{:T(128)}, s32[]{:T(128)}) while((s32[]{:T(128)}, f32[64,64,128]{2,1,0:T(8,128)S(1)}, s32[]{:T(128)}, f32[8,64]{1,0:T(8,128)S(1)}, ...), condition=%wide.region_4.5_spmd.clone, body=%wide.region_3.4_spmd.clone.sunk | while | flops 2097160 | bytes 6292391 | solution.py:26
  345.4 3.8 collective-permute-start
  349.2 42.4 %collective-permute-done = f32[64,64,128]{2,1,0:T(8,128)} collective-permute-done((f32[64,64,128]{2,1,0:T(8,128)S(1)}, f32[64,64,128]{2,1,0:T(8,128)}, u32[]{:S(2)}, u32[]{:S(2)}) %collective-permute-start) | collective-permute-done | bytes 2097184 | tf_op jit(solution)/shard_map/ppermute | solution.py:32
  394.1 176.6 %reduce-scatter.2.cloned.1.call-done = f32[2,64,128]{2,1,0:T(8,128)} async-done(((f32[64,64,128]{2,1,0:T(8,128)}), f32[2,64,128]{2,1,0:T(8,128)}) %reduce-scatter.2.cloned.1.call-update) | async-done | bytes 65552 | tf_op jit(solution)/shard_map/reduce_scatter | solution.py:268
  571.6 41.2 %all-gather.2 = f32[16,64,128]{2,1,0:T(8,128)} all-gather(f32[2,64,128]{2,1,0:T(8,128)S(1)} %multiply_multiply_fusion), channel_id=4, replica_groups=mesh['seq'=8,'roll'=32] {'seq'}, dimensions={0}, use_global_device_ids=true | all-gather | bytes 589824 | tf_op jit(solution)/shard_map/all_gather | solution.py:13
  612.8 12.9 %while.61 = (s32[]{:T(128)}, f32[2,64,128]{2,1,0:T(8,128)S(1)}, s32[]{:T(128)}, f32[8,2]{1,0:T(8,128)}, f32[8,2,64,128]{3,2,1,0:T(8,128)}, /*index=5*/s32[]{:T(128)}, s32[]{:T(128)}, s32[]{:T(128)}, s32[]{:T(128)}) while((s32[]{:T(128)}, f32[2,64,128]{2,1,0:T(8,128)S(1)}, s32[]{:T(128)}, f32[8,2]{1,0:T(8,128)}, ...), condition=%wide.region_7.8_spmd.clone, body=%wide.region_6.7_spmd.clone.sunk | while | flops 65544 | bytes 196799 | solution.py:26
  632.0 40.7 %all-gather.3 = f32[16,64,128]{2,1,0:T(8,128)} all-gather(f32[2,64,128]{2,1,0:T(8,128)S(1)} %fusion.41), channel_id=5, replica_groups=mesh['seq'=8,'roll'=32] {'seq'}, dimensions={0}, use_global_device_ids=true | all-gather | bytes 589824 | tf_op jit(solution)/shard_map/all_gather | solution.py:13
  672.7 18.1 %while.62 = (s32[]{:T(128)}, f32[2,64,128]{2,1,0:T(8,128)}, s32[]{:T(128)}, f32[8,2]{1,0:T(8,128)}, f32[8,2,64,128]{3,2,1,0:T(8,128)}, /*index=5*/s32[]{:T(128)}, s32[]{:T(128)}) while((s32[]{:T(128)}, f32[2,64,128]{2,1,0:T(8,128)}, s32[]{:T(128)}, f32[8,2]{1,0:T(8,128)}, f32[8,2,64,128]{3,2,1,0:T(8,128)}, ...), condition=%wide.region_13.14_spmd.clone, body=%wide.region_12.13_spmd.clone.sunk | while | flops 65540 | bytes 196737 | solution.py:26
  693.1 73.0 %all-gather.11.cloned.1.call-done = f32[64,64,128]{2,1,0:T(8,128)} async-done(((f32[2,64,128]{2,1,0:T(8,128)}), f32[64,64,128]{2,1,0:T(8,128)}) %all-gather.11.cloned.1.call-update) | async-done | bytes 2097168 | tf_op jit(solution)/shard_map/all_gather | solution.py:225
  768.2 2.6 copy.76
  771.7 2.8 fusion.13
  774.5 46.6 %collective-permute-done.1 = f32[64,64,128]{2,1,0:T(8,128)} collective-permute-done((f32[64,64,128]{2,1,0:T(8,128)}, f32[64,64,128]{2,1,0:T(8,128)}, u32[]{:S(2)}, u32[]{:S(2)}) %collective-permute-start.1) | collective-permute-done | bytes 2097184 | tf_op jit(solution)/shard_map/ppermute | solution.py:32
  821.2 3.4 bitcast_add_fusion.4
  830.4 6.1 fusion.8
  838.7 2.6 fusion.11
  842.8 5.2 fusion.20
  861.0 288.0 %all-reduce.4 = bf16[256,4,128]{2,1,0:T(4,128)(2,1)} all-reduce(f32[256,4,128]{2,1,0:T(4,128)} %broadcast_multiply_fusion.1), channel_id=1, replica_groups=mesh['seq'=8,'roll'=32] {'roll'}, use_global_device_ids=true, to_apply=%region_8.9 | all-reduce | flops 131072 | bytes 786432 | tf_op jit(solution)/shard_map/psum | solution.py:275
  1153.7 25.2 %all-gather.13.cloned.1.call-done = f32[512,64,128]{2,1,0:T(8,128)} async-done(((f32[64,64,128]{2,1,0:T(8,128)}), f32[512,64,128]{2,1,0:T(8,128)}) %all-gather.13.cloned.1.call-update) | async-done | bytes 16777232 | tf_op jit(solution)/shard_map/all_gather | solution.py:13
  1178.9 36.5 %while.63 = (s32[]{:T(128)}, f32[64,64,128]{2,1,0:T(8,128)}, s32[]{:T(128)}, f32[8,64]{1,0:T(8,128)}, f32[8,64,64,128]{3,2,1,0:T(8,128)}, /*index=5*/s32[]{:T(128)}, s32[]{:T(128)}) while((s32[]{:T(128)}, f32[64,64,128]{2,1,0:T(8,128)}, s32[]{:T(128)}, f32[8,64]{1,0:T(8,128)}, f32[8,64,64,128]{3,2,1,0:T(8,128)}, ...), condition=%wide.region_19.20_spmd.clone, body=%wide.region_18.19_spmd.clone.sunk | while | flops 2097156 | bytes 6292329 | solution.py:26
  1179.6 3.3 fusion.101
  1183.6 3.9 fusion.101
  1188.2 3.9 fusion.101
  1192.9 3.9 fusion.101
  1197.5 4.0 fusion.101
  1202.2 3.9 fusion.101
  1206.8 3.9 fusion.101
  1211.4 3.9 fusion.101
  1215.4 4.0 multiply_reduce_fusion
  1219.7 5.3 fusion.6
  1228.2 5.7 multiply_reduce_fusion.1
  (235 shorter events, 113.5 us)
Async XLA Ops:
  7.2 620.1 %copy-start = (bf16[256,512]{1,0:T(8,128)(2,1)S(1)}, bf16[256,512]{1,0:T(8,128)(2,1)}, u32[]{:S(2)}) copy-start(bf16[256,512]{1,0:T(8,128)(2,1)} %param.22) | copy-start | bytes 786436
  7.2 319.2 %all-gather.9.cloned.1.call-start = ((), (), s32[]{:S(2)}) async-start(), calls=%async_computation.1 | async-start | bytes 18874368 | tf_op jit(solution)/shard_map/all_gather | solution.py:13
  8.6 6.4 copy-start.27
  8.6 6.4 copy-start.31
  10.0 10.2 copy-start.38
  12.5 5.8 copy-start.43
  15.1 555.6 %reduce-scatter.2.cloned.1.call-start = ((), (), s32[]{:S(2)}) async-start(), calls=%async_computation.2 | async-start | bytes 2162688 | tf_op jit(solution)/shard_map/reduce_scatter | solution.py:268
  16.4 310.0 %copy-start.22 = (f32[256]{0:T(256)}, f32[256]{0:T(256)S(1)}, u32[]{:S(2)}) copy-start(f32[256]{0:T(256)S(1)} %compare_convert_fusion.3) | copy-start | bytes 3076
  18.2 375.7 %copy-start.30 = (f32[2,1]{0,1:T(1,128)}, f32[2,1]{0,1:T(1,128)S(1)}, u32[]{:S(2)}) copy-start(f32[2,1]{0,1:T(1,128)S(1)} %copy.96) | copy-start | bytes 28
  326.4 17.1 %copy-start.39 = (f32[64]{0:T(128)S(1)}, f32[64]{0:T(128)}, u32[]{:S(2)}) copy-start(f32[64]{0:T(128)} %copy-done.38) | copy-start | bytes 772
  345.4 225.3 %copy-start.34 = (f32[2]{0:T(128)S(1)}, f32[2]{0:T(128)}, u32[]{:S(2)}) copy-start(f32[2]{0:T(128)} %get-tuple-element.629) | copy-start | bytes 28
  345.4 46.2 %collective-permute-start = (f32[64,64,128]{2,1,0:T(8,128)S(1)}, f32[64,64,128]{2,1,0:T(8,128)}, u32[]{:S(2)}, u32[]{:S(2)}) collective-permute-start(f32[64,64,128]{2,1,0:T(8,128)S(1)} %fusion.12), channel_id=1, source_target_pairs={{0,224},{1,225},{2,226},{3,227},{4,228},{5,229},{6,230},{7,231},{8... | collective-permute-start | bytes 6291464 | tf_op jit(solution)/shard_map/ppermute | solution.py:32
  349.2 42.5 %copy-start.42 = (f32[16]{0:T(128)S(1)}, f32[16]{0:T(128)}, u32[]{:S(2)}) copy-start(f32[16]{0:T(128)} %get-tuple-element.604) | copy-start | bytes 196
  391.6 374.4 %all-gather.11.cloned.1.call-start = ((), (), s32[]{:S(2)}) async-start(), calls=%async_computation.3 | async-start | bytes 2162688 | tf_op jit(solution)/shard_map/all_gather | solution.py:225
  690.8 80.9 %copy-start.16 = (f32[128,4,16]{0,2,1:T(8,128)S(1)}, f32[128,4,16]{0,2,1:T(8,128)}, u32[]{:S(2)}) copy-start(f32[128,4,16]{0,2,1:T(8,128)} %get-tuple-element.625) | copy-start | bytes 98308
  693.0 485.9 %all-gather.13.cloned.1.call-start = ((), (), s32[]{:S(2)}) async-start(), calls=%async_computation.4 | async-start | bytes 18874368 | tf_op jit(solution)/shard_map/all_gather | solution.py:13
  766.0 55.2 %collective-permute-start.1 = (f32[64,64,128]{2,1,0:T(8,128)}, f32[64,64,128]{2,1,0:T(8,128)}, u32[]{:S(2)}, u32[]{:S(2)}) collective-permute-start(f32[64,64,128]{2,1,0:T(8,128)} %all-gather.11.cloned.1.call-done), channel_id=1, source_target_pairs={{224,0},{225,1},{226,2},{227,3},{228,4},{229,5},{230,6},{231,7},{2... | collective-permute-start | bytes 6291464 | tf_op jit(solution)/shard_map/ppermute | solution.py:32
  771.7 54.6 %copy-start.4 = (bf16[128,4,128]{2,1,0:T(4,128)(2,1)}, bf16[128,4,128]{2,1,0:T(4,128)(2,1)S(1)}, u32[]{:S(2)}) copy-start(bf16[128,4,128]{2,1,0:T(4,128)(2,1)S(1)} %reshape_squeeze.17) | copy-start | bytes 393220
  824.6 5.8 copy-start.32
  826.3 10.2 copy-start.6
  842.8 5.2 copy-start.7
  842.8 7.8 copy-start.11
  848.0 304.4 %copy-start.23 = (f32[256]{0:T(256)S(1)}, f32[256]{0:T(256)}, u32[]{:S(2)}) copy-start(f32[256]{0:T(256)} %copy-done.22) | copy-start | bytes 3076
  1219.7 5.4 copy-start.14
  1219.7 5.4 copy-start.15
  1219.7 5.4 copy-start.17
  1219.7 5.4 copy-start.18
  1219.7 5.4 copy-start.26
  1219.7 5.4 copy-start.41
  1219.7 7.3 copy-start.10
  1219.7 8.5 copy-start.40
  1228.2 7.8 copy-start.1
  (18 other events, 49.8 us)
Sparse Core Ops, SparseCore 0:
  15.2 311.1 all-gather.8
  391.8 178.8 reduce-scatter.1
  693.1 72.8 all-gather.10
  824.8 354.1 all-gather.12
where the time goes:
time: 1250 us; the launch traced here: 1240 us
  waiting for transfers between devices  637 us (51%)
  blocking collectives  403 us (32%)
  other arithmetic  102 us (8%)
  local copies, waits for them, and re-layouts  41.2 us (3%)
  matrix products  37.1 us (3%)
  between operations  17 us (1%)
    all_gather x2, waiting for transfers between devices, prefix(): everything = jax.tree.map(lambda part: lax.all_gather(part, axis), value)  298 us
    psum x1, blocking collectives, local(): grad_b_whole = lax.psum(placed, 'roll')  288 us
    reduce_scatter x1, waiting for transfers between devices, local(): lax.psum_scatter(moved_grad, 'roll', scatter_dimension=0, tiled=True)  177 us
    ppermute x2, waiting for transfers between devices, passed_along(): lax.ppermute(value, axis, [(source, source + steps) for source in range(i...  89.1 us
    all_gather x2, blocking collectives, prefix(): everything = jax.tree.map(lambda part: lax.all_gather(part, axis), value)  81.9 us
    all_gather x1, waiting for transfers between devices, local(): assembled = lax.all_gather(prompt_tail, 'roll', axis=0, tiled=True)  73 us
    select_n x32, other arithmetic, lap(): return jax.tree.map(lambda a, b: jnp.where(reached, a, b), new, before)  67.5 us
    unnamed x1, blocking collectives  32.7 us
  transfers between devices with their start and end apart: 6, of which 6 were waited for; matrix products, arithmetic and copies ran while one was open for 4% of the time, Pallas kernels for 0%

commit v1 on v0

v1 whole, which is shorter than its diff:
```python
import functools

import jax
import jax.numpy as jnp
from jax import lax
from jax.experimental import pallas as pl
from jax.experimental.pallas import tpu as pltpu
from jax.sharding import PartitionSpec as P

MESH = pl.DeviceIdType.MESH
F32 = jnp.float32
BF16 = jnp.bfloat16
HEADS = 64
GROUPS = 4
TOK = 128
PTOK = 256
LANE = 128
PAIRS = 32
PER = 8
ROWS = 1024
EXACT = lax.Precision.HIGHEST


def iota(shape, axis):
    return lax.broadcasted_iota(jnp.int32, shape, axis)


def mm(a, b):
    return lax.dot_general(a, b, (((1,), (0,)), ((), ())), preferred_element_type=F32)


def mm_nt(a, b):
    return lax.dot_general(a, b, (((1,), (1,)), ((), ())), preferred_element_type=F32)


def mm_tn(a, b):
    return lax.dot_general(a, b, (((0,), (0,)), ((), ())), preferred_element_type=F32)


def exact(a, b):
    return lax.dot_general(a, b, (((1,), (0,)), ((), ())), preferred_element_type=F32, precision=EXACT)


def halves(value):
    high = value.astype(BF16)
    return high, (value - high.astype(F32)).astype(BF16)


def columns(first, second, rows, length):
    stacked = jnp.where(iota((rows, length), 0) < 64, first, second)
    return stacked.T


def kernel(
    xp_ref, dtp_ref, bp_ref, x_ref, dt_ref, b_ref, c_ref, rate_ref, skip_ref, gy_ref, len_ref, plen_ref,
    gxp_ref, gbp_ref, gdtp_ref, gx_ref, gb_ref, gc_ref, gdt_ref,
    cum, wrow, step, decay, cot, xw, cw, wx, cb, pooled, dxi, zs, xs, car,
    s_loc, l_loc, s_all, l_all, dec_all, t_out, t_in, e_out, b_out, e_all, b_all,
    p_all, pdec, pdec_all, fork_out, fork_all, enter_p, xw_p, wx_p,
    back, fg_all, fg_out, q_all, gbo, gb_all, go_out, go_all,
    ss_p, rs_p, ss_pd, rs_pd, ss_d, rs_d, ss_s, rs_s, ss_l, rs_l, ss_z, rs_z,
    ss_f, rs_f, ss_b, rs_b, ss_e, rs_e, ss_g, rs_g, ss_q, rs_q, ss_gb, rs_gb, ss_go, rs_go,
):
    s = lax.axis_index("seq")
    r = lax.axis_index("roll")
    z, x = s // 4, s % 4
    y, q = r // 8, r % 8

    def at(seq, roll):
        return {"seq": seq, "roll": roll}

    def copy(src, dst, send, recv, seq, roll):
        return pltpu.make_async_remote_copy(
            src_ref=src, dst_ref=dst, send_sem=send, recv_sem=recv, device_id=at(seq, roll), device_id_type=MESH
        )

    bar = pltpu.get_barrier_semaphore()

    def greet(seq, roll):
        pl.semaphore_signal(bar, inc=1, device_id=at(seq, roll), device_id_type=MESH)

    def greet_plane(d, carry):
        greet(s, lax.rem(r + d, 32))
        return carry

    def greet_seq(d, carry):
        greet(lax.rem(s + d, 8), r)
        return carry

    lax.fori_loop(1, 8, greet_seq, 0)
    lax.fori_loop(1, 32, greet_plane, 0)

    def greet_quarter(k, carry):
        @pl.when(jnp.logical_not((s == y) & (k == y)))
        def _():
            greet(y, k * 8 + q)

        return carry

    lax.fori_loop(0, 4, greet_quarter, 0)

    live = (s * TOK + iota((1, TOK), 1) < len_ref[0]).astype(F32)
    step[...] = dt_ref[...] * live
    logd = -rate_ref[...] * step[...]
    upto = (iota((TOK, TOK), 0) <= iota((TOK, TOK), 1)).astype(F32)
    cum_v = exact(logd, upto)
    end_v = exact(logd, jnp.ones((TOK, TOK), F32))
    cum[...] = cum_v
    decay[...] = jnp.exp(end_v)
    wrow[...] = step[...] * jnp.exp(end_v - cum_v)

    low8 = iota((8, PTOK), 0) < 1
    dtp = jnp.where(low8, dtp_ref[0:1, :], dtp_ref[1:2, :])
    r0 = rate_ref[pl.ds(2 * r, 1), :]
    r1 = rate_ref[pl.ds(2 * r + 1, 1), :]
    ratep = jnp.where(low8, jnp.concatenate([r0, r0], axis=1), jnp.concatenate([r1, r1], axis=1))
    first_live = 8 * PTOK - plen_ref[0]
    live_p = (s * PTOK + iota((1, PTOK), 1) >= first_live).astype(F32)
    step_p = dtp * live_p
    logd_p = -ratep * step_p
    upto_p = (iota((PTOK, PTOK), 0) <= iota((PTOK, PTOK), 1)).astype(F32)
    cum_p = exact(logd_p, upto_p)
    end_p = exact(logd_p, jnp.ones((PTOK, PTOK), F32))
    w_p = step_p * jnp.exp(end_p - cum_p)
    pdec[...] = jnp.exp(end_p[:, 0:LANE])
    wx_p[...] = columns(w_p[0:1, :], w_p[1:2, :], LANE, PTOK)
    xw_p[...] = (xp_ref[...].astype(F32) * wx_p[...]).astype(BF16)
    bp = bp_ref[:, pl.ds(pl.multiple_of(y * LANE, LANE), LANE)]
    p_all[s] = mm_tn(xw_p[...], bp).astype(BF16)
    pdec_all[s] = pdec[...]

    extra = jnp.where(z == 0, 8 - (y == x).astype(jnp.int32), 0)
    pl.semaphore_wait(bar, 38 + extra)

    def p_copy(d):
        return copy(p_all.at[s], p_all.at[s], ss_p.at[d], rs_p.at[s], lax.rem(s + d, 8), r)

    def pd_copy(d):
        return copy(pdec, pdec_all.at[s], ss_pd.at[d], rs_pd.at[s], lax.rem(s + d, 8), r)

    def d_copy(d):
        k = lax.rem(x + d, 4)
        return copy(decay.at[pl.ds(pl.multiple_of(k * 16, 16), 16)], dec_all.at[x], ss_d.at[d], rs_d.at[x], z * 4 + k, r)

    def slice_of(k):
        return pl.ds(pl.multiple_of(k * ROWS, ROWS), ROWS)

    def s_copy(d):
        k = lax.rem(x + d, 4)
        return copy(s_loc.at[slice_of(k)], s_all.at[x], ss_s.at[d], rs_s.at[x], z * 4 + k, r)

    def l_copy(d):
        k = lax.rem(x + d, 4)
        return copy(l_loc.at[slice_of(k)], l_all.at[x], ss_l.at[d], rs_l.at[x], z * 4 + k, r)

    def z_copy():
        return copy(t_out, t_in, ss_z, rs_z, (1 - z) * 4 + x, r)

    def f_copy(d):
        return copy(fork_out, fork_all.at[q], ss_f.at[d], rs_f.at[q], s, lax.rem(r + d, 32))

    def b_copy(d):
        k = lax.rem(x + d, 4)
        return copy(b_out.at[k], b_all.at[slice_of(x)], ss_b.at[d], rs_b.at[x], z * 4 + k, r)

    def e_copy(d):
        k = lax.rem(x + d, 4)
        return copy(e_out.at[k], e_all.at[slice_of(x)], ss_e.at[d], rs_e.at[x], z * 4 + k, r)

    def g_copy(d):
        t = lax.rem(r + d, 32)
        piece = pl.multiple_of(lax.rem(t, 8) * 128 + t // 8 * 32, 32)
        return copy(back.at[pl.ds(piece, 32)], fg_all.at[r], ss_g.at[d], rs_g.at[r], s, t)

    def q_copy(k):
        return copy(fg_out, q_all.at[y], ss_q.at[k], rs_q.at[y], k, x * 8 + q)

    def gb_copy(d):
        t = lax.rem(q + d, 8)
        return copy(gbo.at[pl.ds(pl.multiple_of(t * 32, 32), 32)], gb_all.at[q], ss_gb.at[d], rs_gb.at[q], s, y * 8 + t)

    def go_copy(d):
        return copy(go_out, go_all.at[r], ss_go.at[d], rs_go.at[r], s, lax.rem(r + d, 32))

    def each(first, last, act):
        def body(d, carry):
            act(d)
            return carry

        lax.fori_loop(first, last, body, 0)

    each(1, 8, lambda d: p_copy(d).start())
    each(1, 8, lambda d: pd_copy(d).start())
    each(1, 4, lambda d: d_copy(d).start())
    dec_all[x] = decay[pl.ds(pl.multiple_of(x * 16, 16), 16), :]

    row_live = iota((TOK, LANE), 0) + s * TOK < len_ref[0]

    def lanes(i):
        return pl.ds(pl.multiple_of(i * LANE, LANE), LANE)

    def s_pair(i, c_g):
        cx = columns(cum[pl.ds(2 * i, 1), :], cum[pl.ds(2 * i + 1, 1), :], LANE, TOK)
        ct = jnp.where(row_live, gy_ref[:, lanes(i)].astype(F32), 0.0)
        cot[:, lanes(i)] = ct.astype(BF16)
        weighted = (ct * jnp.exp(cx)).astype(BF16)
        cw[:, lanes(i)] = weighted
        s_loc[lanes(i), :] = mm_tn(weighted, c_g).astype(BF16)

    def l_pair(i, b_g):
        wide = columns(wrow[pl.ds(2 * i, 1), :], wrow[pl.ds(2 * i + 1, 1), :], LANE, TOK)
        wx[:, lanes(i)] = wide
        weighted = (x_ref[:, lanes(i)].astype(F32) * wide).astype(BF16)
        xw[:, lanes(i)] = weighted
        l_loc[lanes(i), :] = mm_tn(weighted, b_g).astype(BF16)

    for d in (2, 1, 3, 0):
        g = lax.rem(x + d, 4)
        c_g = c_ref[:, lanes(g)]
        each(0, PER, lambda i: s_pair(g * PER + i, c_g))
        if d:
            s_copy(d).start()
        else:
            s_all[x] = s_loc[slice_of(x), :]
    for d in (2, 1, 3, 0):
        g = lax.rem(x + d, 4)
        b_g = b_ref[:, lanes(g)]
        each(0, PER, lambda i: l_pair(g * PER + i, b_g))
        if d:
            l_copy(d).start()
        else:
            l_all[x] = l_loc[slice_of(x), :]

    def wait_from(count, mine, make):
        def body(d, carry):
            make(lax.rem(mine + d, count)).wait_recv()
            return carry

        lax.fori_loop(1, count, body, 0)

    wait_from(8, s, lambda k: copy(p_all.at[k], p_all.at[k], ss_p.at[0], rs_p.at[k], s, r))
    wait_from(8, s, lambda k: copy(pdec, pdec_all.at[k], ss_pd.at[0], rs_pd.at[k], s, r))
    top = iota((LANE, LANE), 0) < 64

    zero = jnp.zeros((LANE, LANE), F32)
    enter_p[...] = zero
    fork = p_all[0].astype(F32)
    for k in range(1, 8):
        enter_p[...] = jnp.where(k == s, fork, enter_p[...])
        fork = jnp.where(top, pdec_all[k, 0:1, :], pdec_all[k, 1:2, :]) * fork + p_all[k].astype(F32)

    @pl.when((z == 0) & (y == x))
    def _():
        fork_out[...] = fork.astype(BF16)
        fork_all[q] = fork.astype(BF16)
        each(1, 32, lambda d: f_copy(d).start())

    for g in range(GROUPS):
        cb[g] = mm_nt(c_ref[:, g * LANE : (g + 1) * LANE], b_ref[:, g * LANE : (g + 1) * LANE])
        pooled[g] = zero
    zs[...] = jnp.zeros_like(zs)
    xs[...] = jnp.zeros_like(xs)
    car[...] = jnp.zeros_like(car)
    causal = iota((TOK, TOK), 0) >= iota((TOK, TOK), 1)
    left = iota((TOK, LANE), 1) < 64

    def collect(i, zz, xd):
        z_hi, z_lo = halves(zz)
        row = iota((16, 3 * LANE), 0)
        lane = iota((16, 3 * LANE), 1)
        slot = 2 * lax.rem(i, 4) + (lax.rem(lane, LANE) >= 64).astype(jnp.int32)
        slot = slot + jnp.where(lane >= 2 * LANE, 8, 0)
        pick = (row == slot).astype(F32).astype(BF16)
        sums = mm_nt(pick, jnp.concatenate([z_hi, z_lo, xd.astype(BF16)], axis=1))
        at8 = pl.ds(pl.multiple_of(i // 4 * 8, 8), 8)
        zs[at8, :] = zs[at8, :] + sums[0:8]
        xs[at8, :] = xs[at8, :] + sums[8:16]

    def intra(i):
        g = i // PER
        xi = x_ref[:, lanes(i)]
        ci = cot[:, lanes(i)]
        xf = xi.astype(F32)
        cf = ci.astype(F32)
        both = jnp.concatenate([jnp.where(left, cf, 0.0).astype(BF16), jnp.where(left, 0.0, cf).astype(BF16)], axis=0)
        gx = mm_nt(both, xi)
        cbg = cb[g]
        mixes = []
        total = pooled[g]
        for a in range(2):
            row = cum[pl.ds(2 * i + a, 1), :]
            col = jnp.broadcast_to(row, (TOK, TOK)).T
            seg = jnp.where(causal, jnp.exp(col - row), 0.0) * step[pl.ds(2 * i + a, 1), :]
            total = total + seg * gx[a * TOK : (a + 1) * TOK]
            mixes.append((seg * cbg).astype(BF16))
        pooled[g] = total
        mix = jnp.concatenate(mixes, axis=0)
        dx = mm_tn(mix, both)
        yy = mm(mix, xi)
        yi = jnp.where(left, yy[:TOK], yy[TOK:])
        dxi[:, lanes(i)] = dx
        xd = xf * dx
        collect(i, cf * yi - xd, xd)

    each(0, PAIRS // 2, intra)

    wait_from(4, x, lambda k: copy(decay.at[pl.ds(0, 16)], dec_all.at[k], ss_d.at[0], rs_d.at[k], s, r))
    wait_from(4, x, lambda k: copy(s_all.at[k], s_all.at[k], ss_s.at[0], rs_s.at[k], s, r))

    def head_rows(h):
        return pl.ds(pl.multiple_of(h * 64, 64), 64)

    def backward(start, finish):
        def body(h):
            state = start(head_rows(h))
            for k in (3, 2, 1, 0):
                b_out[k, head_rows(h), :] = state.astype(BF16)
                state = dec_all[k, pl.ds(h, 1), :] * state + s_all[k, head_rows(h), :].astype(F32)
            finish[head_rows(h), :] = state.astype(BF16)

        each(0, 16, body)

    def forward(start, finish):
        def body(h):
            state = start(head_rows(h))
            for k in range(4):
                e_out[k, head_rows(h), :] = state.astype(BF16)
                state = dec_all[k, pl.ds(h, 1), :] * state + l_all[k, head_rows(h), :].astype(F32)
            if finish is not None:
                finish[head_rows(h), :] = state.astype(BF16)

        each(0, 16, body)

    def give_back(out, whole, make):
        for d in (2, 1, 3):
            make(d).start()
        whole[slice_of(x), :] = out[x]

    @pl.when(z == 1)
    def _():
        backward(lambda rows: jnp.zeros((64, LANE), F32), t_out)
        z_copy().start()
        give_back(b_out, b_all, b_copy)

    each(PAIRS // 2, PAIRS, intra)

    wait_from(4, x, lambda k: copy(l_all.at[k], l_all.at[k], ss_l.at[0], rs_l.at[k], s, r))

    @pl.when(z == 0)
    def _():
        def fork_wait(k):
            @pl.when(jnp.logical_not((y == x) & (q == k)))
            def _():
                copy(fork_out, fork_all.at[k], ss_f.at[0], rs_f.at[k], s, r).wait_recv()

        each(0, 8, fork_wait)

        def body(h):
            state = fork_all[h // 2, pl.ds(pl.multiple_of(lax.rem(h, 2) * 64, 64), 64), :].astype(F32)
            for k in range(4):
                e_out[k, head_rows(h), :] = state.astype(BF16)
                state = dec_all[k, pl.ds(h, 1), :] * state + l_all[k, head_rows(h), :].astype(F32)
            t_out[head_rows(h), :] = state.astype(BF16)

        each(0, 16, body)
        z_copy().start()
        z_copy().wait_recv()
        backward(lambda rows: t_in[rows, :].astype(F32), back)
        each(1, 32, lambda d: g_copy(d).start())
        own = pl.multiple_of(q * 128 + y * 32, 32)
        fg_all[r] = back[pl.ds(own, 32), :]
        give_back(b_out, b_all, b_copy)
        give_back(e_out, e_all, e_copy)

    @pl.when(z == 1)
    def _():
        z_copy().wait_recv()
        forward(lambda rows: t_in[rows, :].astype(F32), None)
        give_back(e_out, e_all, e_copy)

    @pl.when(z == 0)
    def _():
        wait_from(32, r, lambda k: copy(fg_all.at[k], fg_all.at[k], ss_g.at[0], rs_g.at[k], s, r))
        total = fg_all[0].astype(F32)
        for k in range(1, 32):
            total = total + fg_all[k].astype(F32)
        fg_out[...] = total

        def q_send(k):
            @pl.when(jnp.logical_not((k == s) & (y == x)))
            def _():
                q_copy(k).start()

        each(0, 8, q_send)

        @pl.when(y == x)
        def _():
            q_all[y] = total

    def part_b(d):
        g = lax.rem(x + d, 4)
        if d:
            copy(b_out.at[0], b_all.at[slice_of(g)], ss_b.at[0], rs_b.at[g], s, r).wait_recv()
        b_g = b_ref[:, lanes(g)]
        wide = pl.ds(pl.multiple_of(g * ROWS, ROWS), ROWS)

        def pair(j):
            i = g * PER + j
            pulled = mm_nt(b_g, b_all[lanes(i), :])
            inter = wx[:, lanes(i)] * pulled
            xd = x_ref[:, lanes(i)].astype(F32) * inter
            grad = dxi[:, lanes(i)] + inter + skip_ref[:, lanes(i)] * cot[:, lanes(i)].astype(F32)
            gx_ref[:, lanes(i)] = grad.astype(BF16)
            collect(i, -xd, xd)
            leave = jnp.sum(xd, axis=0, keepdims=True)
            row = iota((8, LANE), 0)
            slot = 2 * lax.rem(i, 4) + (iota((8, LANE), 1) >= 64).astype(jnp.int32)
            at8 = pl.ds(pl.multiple_of(i // 4 * 8, 8), 8)
            car[at8, :] = car[at8, :] + jnp.where(row == slot, leave, 0.0)

        each(0, PER, pair)
        grad_b = mm_tn(pooled[g].astype(BF16), c_ref[:, lanes(g)]) + mm(xw[:, wide], b_all[wide, :])
        gb_ref[:, lanes(g)] = grad_b.astype(BF16)

    for d in (0, 1, 3, 2):
        part_b(d)

    def q_wait(k):
        @pl.when(jnp.logical_not((s == y) & (k == y)))
        def _():
            copy(fg_out, q_all.at[k], ss_q.at[0], rs_q.at[k], s, r).wait_recv()

    each(0, 4, q_wait)

    q_whole = jnp.concatenate([q_all[k] for k in range(4)], axis=0)
    for k in range(1, 8):
        q_whole = q_whole * jnp.where(k > s, jnp.where(top, pdec_all[k, 0:1, :], pdec_all[k, 1:2, :]), 1.0)
    q_state = q_whole.astype(BF16)
    pulled_p = mm_nt(bp, q_state)
    dx_p = wx_p[...] * pulled_p
    gxp_ref[...] = dx_p.astype(BF16)
    gbo[...] = mm(xw_p[...], q_state).astype(BF16)
    each(1, 8, lambda d: gb_copy(d).start())
    gb_all[q] = gbo[pl.ds(pl.multiple_of(q * 32, 32), 32), :]
    xd_p = xp_ref[...].astype(F32) * dx_p
    xd_hi, xd_lo = halves(xd_p)
    pick = (iota((8, 2 * LANE), 0) == (lax.rem(iota((8, 2 * LANE), 1), LANE) >= 64).astype(jnp.int32)).astype(F32)
    leave_p = mm_nt(pick.astype(BF16), jnp.concatenate([xd_hi, xd_lo], axis=1))
    before = (iota((PTOK, PTOK), 0) < iota((PTOK, PTOK), 1)).astype(F32)
    passed = exact(leave_p, before)
    meet = q_state.astype(F32) * enter_p[...]
    meet = jnp.where(
        iota((8, LANE), 0) < 1,
        jnp.sum(jnp.where(top, meet, 0.0), axis=0, keepdims=True),
        jnp.sum(jnp.where(top, 0.0, meet), axis=0, keepdims=True),
    )
    through = jnp.sum(meet * pdec[...], axis=1, keepdims=True)
    grad_p = live_p * (leave_p / dtp - ratep * (passed + through))
    gdtp_ref[...] = grad_p[0:2, :]

    def part_e(d):
        g = lax.rem(x + d, 4)
        if d:
            copy(e_out.at[0], e_all.at[slice_of(g)], ss_e.at[0], rs_e.at[g], s, r).wait_recv()
        c_g = c_ref[:, lanes(g)]
        wide = pl.ds(pl.multiple_of(g * ROWS, ROWS), ROWS)

        def pair(j):
            i = g * PER + j
            entry = e_all[lanes(i), :]
            seen = mm_nt(c_g, entry)
            zz = cw[:, lanes(i)].astype(F32) * seen
            collect(i, zz, zz)
            prod = entry.astype(F32) * b_all[lanes(i), :].astype(F32)
            row = iota((8, LANE), 0)
            slot = 2 * lax.rem(i, 4)
            one = jnp.sum(jnp.where(top, prod, 0.0), axis=0, keepdims=True) * decay[pl.ds(2 * i, 1), :]
            two = jnp.sum(jnp.where(top, 0.0, prod), axis=0, keepdims=True) * decay[pl.ds(2 * i + 1, 1), :]
            at8 = pl.ds(pl.multiple_of(i // 4 * 8, 8), 8)
            add = jnp.where(row == slot, one, 0.0) + jnp.where(row == slot + 1, two, 0.0)
            car[at8, :] = car[at8, :] + add

        each(0, PER, pair)
        grad_c = mm(pooled[g].astype(BF16), b_ref[:, lanes(g)]) + mm(cw[:, wide], e_all[wide, :])
        gc_ref[:, lanes(g)] = grad_c.astype(BF16)

    keep = xs[...]
    for d in (0, 1, 3, 2):
        part_e(d)
    carried = jnp.sum(car[...], axis=1, keepdims=True)
    onward = (iota((TOK, TOK), 0) >= iota((TOK, TOK), 1)).astype(F32)
    grad_log = exact(zs[...], onward) + carried
    gdt_ref[...] = live * (keep / dt_ref[...] - rate_ref[...] * grad_log)

    wait_from(8, q, lambda k: copy(gb_all.at[k], gb_all.at[k], ss_gb.at[0], rs_gb.at[k], s, r))
    total = gb_all[0].astype(F32)
    for k in range(1, 8):
        total = total + gb_all[k].astype(F32)
    go_out[...] = total.astype(BF16)
    go_all[r] = total.astype(BF16)
    each(1, 32, lambda d: go_copy(d).start())
    wait_from(32, r, lambda k: copy(go_out, go_all.at[k], ss_go.at[0], rs_go.at[k], s, r))
    for k in range(32):
        gbp_ref[(k % 8) * 32 : (k % 8) * 32 + 32, (k // 8) * LANE : (k // 8 + 1) * LANE] = go_all[k]

    each(1, 8, lambda d: p_copy(d).wait_send())
    each(1, 8, lambda d: pd_copy(d).wait_send())
    for make in (d_copy, s_copy, l_copy, b_copy, e_copy):
        each(1, 4, lambda d: make(d).wait_send())
    z_copy().wait_send()
    each(1, 8, lambda d: gb_copy(d).wait_send())
    each(1, 32, lambda d: go_copy(d).wait_send())

    @pl.when((z == 0) & (y == x))
    def _():
        each(1, 32, lambda d: f_copy(d).wait_send())

    @pl.when(z == 0)
    def _():
        each(1, 32, lambda d: g_copy(d).wait_send())

        def q_sent(k):
            @pl.when(jnp.logical_not((k == s) & (y == x)))
            def _():
                q_copy(k).wait_send()

        each(0, 8, q_sent)


def local(
    x_prompt, dt_prompt, b_prompt, x_roll, dt_roll, b_roll, c_roll, rate, skip, grad_y, roll_len, prompt_len
):
    rate_b = jnp.broadcast_to(rate[:, None], (HEADS, LANE))
    skip_b = jnp.repeat(skip, 64)[None]
    vmem = pl.BlockSpec(memory_space=pltpu.VMEM)
    smem = pl.BlockSpec(memory_space=pltpu.SMEM)
    V = pltpu.VMEM
    dma = pltpu.SemaphoreType.DMA
    wide = HEADS * 64
    out = pl.pallas_call(
        kernel,
        name="mixer_backward",
        out_shape=(
            jax.ShapeDtypeStruct((PTOK, LANE), BF16),
            jax.ShapeDtypeStruct((PTOK, 512), BF16),
            jax.ShapeDtypeStruct((2, PTOK), F32),
            jax.ShapeDtypeStruct((TOK, wide), BF16),
            jax.ShapeDtypeStruct((TOK, 512), BF16),
            jax.ShapeDtypeStruct((TOK, 512), BF16),
            jax.ShapeDtypeStruct((HEADS, TOK), F32),
        ),
        in_specs=[vmem] * 10 + [smem] * 2,
        out_specs=(vmem,) * 7,
        scratch_shapes=[
            V((HEADS, TOK), F32), V((HEADS, TOK), F32), V((HEADS, TOK), F32), V((HEADS, LANE), F32),
            V((TOK, wide), BF16), V((TOK, wide), BF16), V((TOK, wide), BF16), V((TOK, wide), F32),
            V((GROUPS, TOK, TOK), F32), V((GROUPS, TOK, TOK), F32), V((TOK, wide), F32),
            V((HEADS, TOK), F32), V((HEADS, TOK), F32), V((HEADS, LANE), F32),
            V((wide, LANE), BF16), V((wide, LANE), BF16), V((4, ROWS, LANE), BF16), V((4, ROWS, LANE), BF16),
            V((4, 16, LANE), F32), V((ROWS, LANE), BF16), V((ROWS, LANE), BF16),
            V((4, ROWS, LANE), BF16), V((4, ROWS, LANE), BF16), V((wide, LANE), BF16), V((wide, LANE), BF16),
            V((8, LANE, LANE), BF16), V((8, LANE), F32), V((8, 8, LANE), F32), V((LANE, LANE), BF16),
            V((8, LANE, LANE), BF16), V((LANE, LANE), F32), V((PTOK, LANE), BF16), V((PTOK, LANE), F32),
            V((ROWS, LANE), BF16), V((32, 32, LANE), BF16), V((32, LANE), F32), V((4, 32, LANE), F32),
            V((PTOK, LANE), BF16), V((8, 32, LANE), BF16), V((32, LANE), BF16), V((32, 32, LANE), BF16),
            dma((8,)), dma((8,)), dma((8,)), dma((8,)), dma((4,)), dma((4,)), dma((4,)), dma((4,)),
            dma((4,)), dma((4,)), dma, dma,
            dma((32,)), dma((8,)), dma((4,)), dma((4,)), dma((4,)), dma((4,)), dma((32,)), dma((32,)),
            dma((8,)), dma((4,)), dma((8,)), dma((8,)), dma((32,)), dma((32,)),
        ],
        compiler_params=pltpu.CompilerParams(
            collective_id=0, has_side_effects=True, vmem_limit_bytes=48 * 1024 * 1024
        ),
        cost_estimate=pl.CostEstimate(flops=1_500_000_000, bytes_accessed=6_000_000, transcendentals=2_000_000),
    )(
        x_prompt, dt_prompt, b_prompt, x_roll[0], dt_roll[0], b_roll[0], c_roll[0], rate_b, skip_b, grad_y[0],
        roll_len, prompt_len,
    )
    gxp, gbp, gdtp, gx, gb, gc, gdt = out
    return gxp, gbp, gdtp, gx[None], gb[None], gc[None], gdt[None]


def solution(mesh):
    in_specs = (
        P("seq", "roll"), P("roll", "seq"), P("seq", None), P("roll", "seq", None), P("roll", None, "seq"),
        P("roll", "seq", None), P("roll", "seq", None), P(), P(), P("roll", "seq", None), P("roll"), P(),
    )
    out_specs = (
        P("seq", "roll"), P("seq", None), P("roll", "seq"), P("roll", "seq", None), P("roll", "seq", None),
        P("roll", "seq", None), P("roll", None, "seq"),
    )
    return jax.shard_map(local, mesh=mesh, in_specs=in_specs, out_specs=out_specs, check_vma=False)
```

time: 1250 us -> 130 us (0.10)
  waiting for transfers between devices: 637 us -> 0 us
  blocking collectives: 403 us -> 0 us
  Pallas kernels: 0 us -> 115 us
  other arithmetic: 102 us -> 0 us
  matrix products: 37.1 us -> 0 us
  local copies, waits for them, and re-layouts: 41.2 us -> 12.2 us
  between operations: 17 us -> 2 us
    all_gather x3 -> x0, waiting for transfers between devices: 371 us -> none  [the longest x2 298 us: prefix(): everything = jax.tree.map(lambda part: lax.all_gather(part, axis), value)]
    psum x1 -> x0, blocking collectives: 288 us -> none  [local(): grad_b_whole = lax.psum(placed, 'roll')]
    reduce_scatter x1 -> x0, waiting for transfers between devices: 177 us -> none  [local(): lax.psum_scatter(moved_grad, 'roll', scatter_dimension=0, tiled=True)]
    pallas_call x0 -> x1, Pallas kernels: none -> 115 us  [local(): pl.pallas_call(kernel, name='mixer_backward', out_shape=(jax.ShapeDtypeSt...]
    ppermute x2 -> x0, waiting for transfers between devices: 89.1 us -> none  [passed_along(): lax.ppermute(value, axis, [(source, source + steps) for source in range(i...]
    all_gather x2 -> x0, blocking collectives: 81.9 us -> none  [prefix(): everything = jax.tree.map(lambda part: lax.all_gather(part, axis), value)]
    select_n x32 -> x0, other arithmetic: 67.5 us -> none  [lap(): return jax.tree.map(lambda a, b: jnp.where(reached, a, b), new, before)]
    dot_general x13 -> x0, matrix products: 37.1 us -> none  [the longest x11 30.8 us: exact_product(): jnp.einsum(spec, *[operand.astype(jnp.float32) for operand in operands],...]
  transfers between devices with their start and end apart: 6 -> 0, of which waited for: 6 -> 0; matrix products, arithmetic and copies ran while one was open for 4% -> 0% of each run, Pallas kernels for 0% -> 0%
where the time goes in v1:
time: 130 us
  Pallas kernels  115 us (88%)
  local copies, waits for them, and re-layouts  12.2 us (9%)
  between operations  2 us (2%)
    pallas_call x1, Pallas kernels, local(): pl.pallas_call(kernel, name='mixer_backward', out_shape=(jax.ShapeDtypeSt...  115 us
    unnamed x23, local copies, waits for them, and re-layouts  10.7 us

profile of v1, /device:TPU:1, one launch (start us, length us, event | category | flops | bytes accessed | tf_op | source)
XLA Modules:
  0.0 129.6 jit_solution(4779614169328259032)
XLA Ops:
  0.6 0.0 copy-start.5
  2.0 0.7 broadcast_in_dim.21.rate_ref
  2.7 0.7 broadcast_in_dim.22
  3.4 0.0 copy-start.6
  3.4 0.0 copy-start.7
  3.4 0.1 broadcast_in_dim_reshape.3.skip_ref
  3.5 0.0 copy-done.5
  3.5 0.7 copy-done.6
  4.2 0.0 copy-done.7
  4.2 0.0 copy-start
  4.2 1.2 copy-done
  5.4 0.0 copy-start.1
  5.4 1.2 copy-done.1
  6.6 0.0 copy-start.2
  6.6 0.9 copy-done.2
  7.6 0.0 copy-start.3
  7.6 0.9 copy-done.3
  8.5 0.0 copy-start.4
  8.5 0.9 copy-done.4
  9.4 115.4 %mixer_backward.1 = (bf16[256,128]{1,0:T(8,128)(2,1)S(1)}, bf16[256,512]{1,0:T(8,128)(2,1)S(1)}, f32[2,256]{1,0:T(2,128)S(1)}, bf16[128,4096]{1,0:T(8,128)(2,1)S...) custom-call(bf16[256,128]{1,0:T(8,128)(2,1)S(1)} %copy-done.5, ...), custom_call_target="tpu_custom_call" | custom-call | flops 1500000000 | bytes 6000000 | tf_op jit(solution)/shard_map/mixer_backward/pallas_call | solution.py:540
  124.8 0.6 copy.28
  125.4 0.7 copy.29
  126.1 0.6 copy.30
  126.7 1.0 copy.31
  127.7 0.7 copy.32
  128.3 0.7 copy.33
  129.0 0.6 copy.34
Async XLA Ops:
  0.6 2.9 %copy-start.5 = (bf16[256,128]{1,0:T(8,128)(2,1)S(1)}, bf16[256,128]{1,0:T(8,128)(2,1)}, u32[]{:S(2)}) copy-start(bf16[256,128]{1,0:T(8,128)(2,1)} %xp_ref.1) | copy-start | bytes 196612
  3.4 0.8 copy-start.6
  3.4 0.8 copy-start.7
  4.2 1.2 copy-start
  5.4 1.2 copy-start.1
  6.6 0.9 copy-start.2
  7.6 0.9 copy-start.3
  8.5 0.9 copy-start.4

commit v2 on v1

v2 whole, which is shorter than its diff:
```python
import functools

import jax
import jax.numpy as jnp
from jax import lax
from jax.experimental import pallas as pl
from jax.experimental.pallas import tpu as pltpu
from jax.sharding import PartitionSpec as P

MESH = pl.DeviceIdType.MESH
F32 = jnp.float32
BF16 = jnp.bfloat16
HEADS = 64
GROUPS = 4
TOK = 128
PTOK = 256
LANE = 128
PAIRS = 32
PER = 8
ROWS = 1024
EXACT = lax.Precision.HIGHEST


def iota(shape, axis):
    return lax.broadcasted_iota(jnp.int32, shape, axis)


def mm(a, b):
    return lax.dot_general(a, b, (((1,), (0,)), ((), ())), preferred_element_type=F32)


def mm_nt(a, b):
    return lax.dot_general(a, b, (((1,), (1,)), ((), ())), preferred_element_type=F32)


def mm_tn(a, b):
    return lax.dot_general(a, b, (((0,), (0,)), ((), ())), preferred_element_type=F32)


def exact(a, b):
    return lax.dot_general(a, b, (((1,), (0,)), ((), ())), preferred_element_type=F32, precision=EXACT)


def halves(value):
    high = value.astype(BF16)
    return high, (value - high.astype(F32)).astype(BF16)


def columns(first, second, rows, length):
    stacked = jnp.where(iota((rows, length), 0) < 64, first, second)
    return stacked.T


def each(first, last, act, unroll=1):
    def body(n, carry):
        for k in range(unroll):
            act(first + n * unroll + k)
        return carry

    lax.fori_loop(0, (last - first) // unroll, body, 0)


def kernel(
    xp_hbm, dtp_hbm, bp_hbm, x_hbm, dt_hbm, b_hbm, c_hbm, gy_hbm, rate_ref, skip_ref, len_ref, plen_ref,
    gxp_hbm, gbp_hbm, gdtp_hbm, gx_hbm, gb_hbm, gc_hbm, gdt_hbm,
    xp_ref, dtp_ref, bp_ref, x_ref, dt_ref, b_ref, c_ref, gy_ref,
    gxp_ref, gbp_ref, gdtp_ref, gx_ref, gb_ref, gc_ref, gdt_ref,
    rates, cum, wrow, step, decay, cot, xw, cw, wx, cb, pooled, dxi, zs, xs, car,
    s_loc, l_loc, s_all, l_all, dec_all, t_out, t_in, e_out, b_out, e_all, b_all,
    p_all, pdec, pdec_all, fork_all, enter_p, xw_p, wx_p,
    back, fg_all, fg_out, q_all, gbo, gb_all, go_all,
    in_sem, out_sem, ss_p, rs_p, ss_pd, rs_pd, ss_d, rs_d, ss_s, rs_s, ss_l, rs_l, ss_z, rs_z,
    ss_fy, ss_fr, rs_f, ss_b, rs_b, ss_e, rs_e, ss_g, rs_g, ss_q, rs_q, ss_gb, rs_gb, ss_gr, rs_gr, ss_gy, rs_gy,
):
    s = lax.axis_index("seq")
    r = lax.axis_index("roll")
    z, x = s // 4, s % 4
    y, q = r // 8, r % 8

    loads = [
        pltpu.make_async_copy(src, dst, in_sem.at[n])
        for n, (src, dst) in enumerate(
            (
                (dt_hbm, dt_ref), (gy_hbm, gy_ref), (c_hbm, c_ref), (dtp_hbm, dtp_ref), (xp_hbm, xp_ref),
                (bp_hbm, bp_ref), (x_hbm, x_ref), (b_hbm, b_ref),
            )
        )
    ]
    for load in loads:
        load.start()

    def at(seq, roll):
        return {"seq": seq, "roll": roll}

    def copy(src, dst, send, recv, seq, roll):
        return pltpu.make_async_remote_copy(
            src_ref=src, dst_ref=dst, send_sem=send, recv_sem=recv, device_id=at(seq, roll), device_id_type=MESH
        )

    bar = pltpu.get_barrier_semaphore()

    def greet(seq, roll):
        pl.semaphore_signal(bar, inc=1, device_id=at(seq, roll), device_id_type=MESH)

    def greet_quarter(k):
        @pl.when(jnp.logical_not((s == k // 4 * 4 + y) & (y == k % 4)))
        def _():
            greet(k // 4 * 4 + y, k % 4 * 8 + q)

    each(1, 8, lambda d: greet(lax.rem(s + d, 8), r))
    each(1, 32, lambda d: greet(s, lax.rem(r + d, 32)))
    each(0, 8, greet_quarter)

    for j in range(HEADS // 8):
        rows8 = jnp.full((8, LANE), rate_ref[8 * j], F32)
        for k in range(1, 8):
            rows8 = jnp.where(iota((8, LANE), 0) == k, rate_ref[8 * j + k], rows8)
        rates[8 * j : 8 * j + 8, :] = rows8
    live = (s * TOK + iota((1, TOK), 1) < len_ref[0]).astype(F32)
    loads[0].wait()
    step[...] = dt_ref[...] * live
    logd = -rates[...] * step[...]
    upto = (iota((TOK, TOK), 0) <= iota((TOK, TOK), 1)).astype(F32)
    cum_v = exact(logd, upto)
    end_v = exact(logd, jnp.ones((TOK, TOK), F32))
    cum[...] = cum_v
    decay[...] = jnp.exp(end_v)
    wrow[...] = step[...] * jnp.exp(end_v - cum_v)

    def slice_of(k):
        return pl.ds(pl.multiple_of(k * ROWS, ROWS), ROWS)

    def lanes(i):
        return pl.ds(pl.multiple_of(i * LANE, LANE), LANE)

    def p_copy(d):
        return copy(p_all.at[s], p_all.at[s], ss_p.at[d], rs_p.at[s], lax.rem(s + d, 8), r)

    def pd_copy(d):
        return copy(pdec, pdec_all.at[s], ss_pd.at[d], rs_pd.at[s], lax.rem(s + d, 8), r)

    def d_copy(d):
        to = lax.rem(s + d, 8)
        part = pl.ds(pl.multiple_of(to % 4 * 16, 16), 16)
        return copy(decay.at[part], dec_all.at[s], ss_d.at[d], rs_d.at[s], to, r)

    def s_copy(d):
        k = lax.rem(x + d, 4)
        return copy(s_loc.at[slice_of(k)], s_all.at[x], ss_s.at[d], rs_s.at[x], z * 4 + k, r)

    def l_copy(d):
        k = lax.rem(x + d, 4)
        return copy(l_loc.at[slice_of(k)], l_all.at[x], ss_l.at[d], rs_l.at[x], z * 4 + k, r)

    def z_copy():
        return copy(t_out, t_in, ss_z, rs_z, (1 - z) * 4 + x, r)

    def fy_copy(d):
        return copy(fork_all.at[q], fork_all.at[q], ss_fy.at[d], rs_f.at[q], s, lax.rem(r + 8 * d, 32))

    def fr_copy(d):
        return copy(fork_all.at[q], fork_all.at[q], ss_fr.at[d], rs_f.at[q], s, y * 8 + lax.rem(q + d, 8))

    def b_copy(d):
        k = lax.rem(x + d, 4)
        return copy(b_out.at[k], b_all.at[slice_of(x)], ss_b.at[d], rs_b.at[x], z * 4 + k, r)

    def e_copy(d):
        k = lax.rem(x + d, 4)
        return copy(e_out.at[k], e_all.at[slice_of(x)], ss_e.at[d], rs_e.at[x], z * 4 + k, r)

    def g_copy(d):
        t = lax.rem(r + d, 32)
        piece = pl.multiple_of(lax.rem(t, 8) * 128 + t // 8 * 32, 32)
        return copy(back.at[pl.ds(piece, 32)], fg_all.at[r], ss_g.at[d], rs_g.at[r], s, t)

    def q_copy(k):
        return copy(fg_out, q_all.at[z * 4 + y], ss_q.at[k], rs_q.at[z * 4 + y], k, x * 8 + q)

    def gb_copy(d):
        t = lax.rem(q + d, 8)
        return copy(gbo.at[pl.ds(pl.multiple_of(t * 32, 32), 32)], gb_all.at[q], ss_gb.at[d], rs_gb.at[q], s, y * 8 + t)

    def gr_copy(d):
        return copy(go_all.at[r], go_all.at[r], ss_gr.at[d], rs_gr.at[q], s, y * 8 + lax.rem(q + d, 8))

    def gy_copy(d):
        block = go_all.at[pl.ds(pl.multiple_of(y * 8, 8), 8)]
        return copy(block, block, ss_gy.at[d], rs_gy.at[y], s, lax.rem(r + 8 * d, 32))

    def wait_from(count, mine, make):
        each(1, count, lambda d: make(lax.rem(mine + d, count)).wait_recv())

    row_live = iota((TOK, LANE), 0) + s * TOK < len_ref[0]
    left = iota((TOK, LANE), 1) < 64
    top = iota((LANE, LANE), 0) < 64
    zero = jnp.zeros((LANE, LANE), F32)

    def s_pair(i, c_g):
        cx = columns(cum[pl.ds(2 * i, 1), :], cum[pl.ds(2 * i + 1, 1), :], LANE, TOK)
        ct = jnp.where(row_live, gy_ref[:, lanes(i)].astype(F32), 0.0)
        cot[:, lanes(i)] = ct.astype(BF16)
        weighted = (ct * jnp.exp(cx)).astype(BF16)
        cw[:, lanes(i)] = weighted
        s_loc[lanes(i), :] = mm_tn(weighted, c_g).astype(BF16)

    def l_pair(i, b_g):
        wide = columns(wrow[pl.ds(2 * i, 1), :], wrow[pl.ds(2 * i + 1, 1), :], LANE, TOK)
        wx[:, lanes(i)] = wide
        weighted = (x_ref[:, lanes(i)].astype(F32) * wide).astype(BF16)
        xw[:, lanes(i)] = weighted
        l_loc[lanes(i), :] = mm_tn(weighted, b_g).astype(BF16)

    loads[1].wait()
    loads[2].wait()
    for d in (2, 1, 3, 0):
        g = lax.rem(x + d, 4)
        c_g = c_ref[:, lanes(g)]
        each(0, PER, lambda i: s_pair(g * PER + i, c_g), 4)
        if d == 2:
            pl.semaphore_wait(bar, 46 - (y == x).astype(jnp.int32))
        if d:
            s_copy(d).start()
        else:
            s_all[x] = s_loc[slice_of(x), :]
    each(1, 8, lambda d: d_copy(d).start())
    dec_all[s] = decay[pl.ds(pl.multiple_of(x * 16, 16), 16), :]

    for n in (3, 4, 5):
        loads[n].wait()
    low8 = iota((8, PTOK), 0) < 1
    dtp = jnp.where(low8, dtp_ref[0:1, :], dtp_ref[1:2, :])
    ratep = jnp.where(low8, rate_ref[2 * r], rate_ref[2 * r + 1])
    first_live = 8 * PTOK - plen_ref[0]
    live_p = (s * PTOK + iota((1, PTOK), 1) >= first_live).astype(F32)
    step_p = dtp * live_p
    logd_p = -ratep * step_p
    upto_p = (iota((PTOK, PTOK), 0) <= iota((PTOK, PTOK), 1)).astype(F32)
    cum_p = exact(logd_p, upto_p)
    end_p = exact(logd_p, jnp.ones((PTOK, PTOK), F32))
    w_p = step_p * jnp.exp(end_p - cum_p)
    pdec[...] = jnp.exp(end_p[:, 0:LANE])
    wx_p[...] = columns(w_p[0:1, :], w_p[1:2, :], LANE, PTOK)
    xw_p[...] = (xp_ref[...].astype(F32) * wx_p[...]).astype(BF16)
    bp = bp_ref[:, lanes(y)]
    p_all[s] = mm_tn(xw_p[...], bp).astype(BF16)
    pdec_all[s] = pdec[...]
    each(1, 8, lambda d: p_copy(d).start())
    each(1, 8, lambda d: pd_copy(d).start())

    loads[6].wait()
    loads[7].wait()
    for g in range(GROUPS):
        b_g = b_ref[:, g * LANE : (g + 1) * LANE]
        each(0, PER, lambda i: l_pair(g * PER + i, b_g), 4)
    l_all[x] = l_loc[slice_of(x), :]

    for g in range(GROUPS):
        cb[g] = mm_nt(c_ref[:, g * LANE : (g + 1) * LANE], b_ref[:, g * LANE : (g + 1) * LANE])
        pooled[g] = zero
    zs[...] = jnp.zeros_like(zs)
    xs[...] = jnp.zeros_like(xs)
    car[...] = jnp.zeros_like(car)
    causal = iota((TOK, TOK), 0) >= iota((TOK, TOK), 1)

    def collect(i, zz, xd):
        z_hi, z_lo = halves(zz)
        row = iota((16, 3 * LANE), 0)
        lane = iota((16, 3 * LANE), 1)
        slot = 2 * lax.rem(i, 4) + (lax.rem(lane, LANE) >= 64).astype(jnp.int32)
        slot = slot + jnp.where(lane >= 2 * LANE, 8, 0)
        pick = (row == slot).astype(F32).astype(BF16)
        sums = mm_nt(pick, jnp.concatenate([z_hi, z_lo, xd.astype(BF16)], axis=1))
        at8 = pl.ds(pl.multiple_of(i // 4 * 8, 8), 8)
        zs[at8, :] = zs[at8, :] + sums[0:8]
        xs[at8, :] = xs[at8, :] + sums[8:16]

    def intra(i):
        g = i // PER
        xi = x_ref[:, lanes(i)]
        ci = cot[:, lanes(i)]
        xf = xi.astype(F32)
        cf = ci.astype(F32)
        both = jnp.concatenate([jnp.where(left, cf, 0.0).astype(BF16), jnp.where(left, 0.0, cf).astype(BF16)], axis=0)
        gx = mm_nt(both, xi)
        cbg = cb[g]
        mixes = []
        total = pooled[g]
        for a in range(2):
            row = cum[pl.ds(2 * i + a, 1), :]
            col = jnp.broadcast_to(row, (TOK, TOK)).T
            seg = jnp.where(causal, jnp.exp(col - row), 0.0) * step[pl.ds(2 * i + a, 1), :]
            total = total + seg * gx[a * TOK : (a + 1) * TOK]
            mixes.append((seg * cbg).astype(BF16))
        pooled[g] = total
        mix = jnp.concatenate(mixes, axis=0)
        dx = mm_tn(mix, both)
        yy = mm(mix, xi)
        yi = jnp.where(left, yy[:TOK], yy[TOK:])
        dxi[:, lanes(i)] = dx
        xd = xf * dx
        collect(i, cf * yi - xd, xd)

    each(0, 8, intra)

    wait_from(8, s, lambda k: copy(p_all.at[k], p_all.at[k], ss_p.at[0], rs_p.at[k], s, r))
    wait_from(8, s, lambda k: copy(pdec, pdec_all.at[k], ss_pd.at[0], rs_pd.at[k], s, r))
    enter_p[...] = zero
    fork = p_all[0].astype(F32)
    for k in range(1, 8):
        enter_p[...] = jnp.where(k == s, fork, enter_p[...])
        fork = jnp.where(top, pdec_all[k, 0:1, :], pdec_all[k, 1:2, :]) * fork + p_all[k].astype(F32)

    @pl.when((z == 0) & (y == x))
    def _():
        fork_all[q] = fork.astype(BF16)
        each(1, 4, lambda d: fy_copy(d).start())
        each(1, 8, lambda d: fr_copy(d).start())

    each(1, 4, lambda d: s_copy(d).wait_send())
    for d in (2, 1, 3):
        l_copy(d).start()
    each(8, 12, intra)

    def fork_slot(k):
        return copy(fork_all.at[k], fork_all.at[k], ss_fr.at[0], rs_f.at[k], s, r)

    @pl.when((z == 0) & (y != x))
    def _():
        fork_slot(q).wait_recv()
        each(1, 8, lambda d: fr_copy(d).start())

    wait_from(8, s, lambda k: copy(decay.at[pl.ds(0, 16)], dec_all.at[k], ss_d.at[0], rs_d.at[k], s, r))
    wait_from(4, x, lambda k: copy(s_all.at[k], s_all.at[k], ss_s.at[0], rs_s.at[k], s, r))

    def head_rows(h):
        return pl.ds(pl.multiple_of(h * 64, 64), 64)

    def give_back(out, whole, make):
        for d in (2, 1, 3):
            make(d).start()
        whole[slice_of(x), :] = out[x]

    def give_pieces():
        each(1, 32, lambda d: g_copy(d).start())
        fg_all[r] = back[pl.ds(pl.multiple_of(q * 128 + y * 32, 32), 32), :]

    @pl.when(z == 1)
    def _():
        def body(h):
            rows = head_rows(h)
            state = jnp.zeros((64, LANE), F32)
            for k in (3, 2, 1, 0):
                b_out[k, rows, :] = state.astype(BF16)
                state = dec_all[4 + k, pl.ds(h, 1), :] * state + s_all[k, rows, :].astype(F32)
            t_out[rows, :] = state.astype(BF16)
            for k in range(4):
                state = dec_all[k, pl.ds(h, 1), :] * state
            back[rows, :] = state.astype(BF16)

        each(0, 16, body)
        z_copy().start()
        give_pieces()
        give_back(b_out, b_all, b_copy)

    @pl.when(z == 0)
    def _():
        def body(h):
            rows = head_rows(h)
            state = s_all[3, rows, :].astype(F32)
            for k in (2, 1, 0):
                state = dec_all[k, pl.ds(h, 1), :] * state + s_all[k, rows, :].astype(F32)
            back[rows, :] = state.astype(BF16)

        each(0, 16, body)
        give_pieces()

    each(12, 24, intra)

    wait_from(32, r, lambda k: copy(fg_all.at[k], fg_all.at[k], ss_g.at[0], rs_g.at[k], s, r))
    total = fg_all[0].astype(F32)
    for k in range(1, 32):
        total = total + fg_all[k].astype(F32)
    fg_out[...] = total

    def q_send(k):
        @pl.when(jnp.logical_not((k == s) & (y == x)))
        def _():
            q_copy(k).start()

    each(0, 8, q_send)

    @pl.when(y == x)
    def _():
        q_all[z * 4 + y] = total

    each(24, 32, intra)

    @pl.when(z == 0)
    def _():
        z_copy().wait_recv()

        def body(h):
            rows = head_rows(h)
            state = t_in[rows, :].astype(F32)
            for k in (3, 2, 1, 0):
                b_out[k, rows, :] = state.astype(BF16)
                if k:
                    state = dec_all[k, pl.ds(h, 1), :] * state + s_all[k, rows, :].astype(F32)

        each(0, 16, body)
        give_back(b_out, b_all, b_copy)

    wait_from(4, x, lambda k: copy(l_all.at[k], l_all.at[k], ss_l.at[0], rs_l.at[k], s, r))

    @pl.when(z == 0)
    def _():
        wait_from(8, q, fork_slot)

        def body(h):
            rows = head_rows(h)
            state = fork_all[h // 2, pl.ds(pl.multiple_of(lax.rem(h, 2) * 64, 64), 64), :].astype(F32)
            for k in range(4):
                e_out[k, rows, :] = state.astype(BF16)
                state = dec_all[k, pl.ds(h, 1), :] * state + l_all[k, rows, :].astype(F32)
            t_out[rows, :] = state.astype(BF16)

        each(0, 16, body)
        z_copy().start()
        give_back(e_out, e_all, e_copy)

    def q_wait(k):
        @pl.when(jnp.logical_not((s == k // 4 * 4 + y) & (y == k % 4)))
        def _():
            copy(fg_out, q_all.at[k], ss_q.at[0], rs_q.at[k], s, r).wait_recv()

    each(0, 8, q_wait)
    q_whole = jnp.concatenate([q_all[k] + q_all[4 + k] for k in range(4)], axis=0)
    for k in range(1, 8):
        q_whole = q_whole * jnp.where(k > s, jnp.where(top, pdec_all[k, 0:1, :], pdec_all[k, 1:2, :]), 1.0)
    q_state = q_whole.astype(BF16)
    pulled_p = mm_nt(bp, q_state)
    dx_p = wx_p[...] * pulled_p
    gxp_ref[...] = dx_p.astype(BF16)
    gbo[...] = mm(xw_p[...], q_state)
    each(1, 8, lambda d: gb_copy(d).start())
    gb_all[q] = gbo[pl.ds(pl.multiple_of(q * 32, 32), 32), :]
    xd_p = xp_ref[...].astype(F32) * dx_p
    xd_hi, xd_lo = halves(xd_p)
    pick = (iota((8, 2 * LANE), 0) == (lax.rem(iota((8, 2 * LANE), 1), LANE) >= 64).astype(jnp.int32)).astype(F32)
    leave_p = mm_nt(pick.astype(BF16), jnp.concatenate([xd_hi, xd_lo], axis=1))
    before = (iota((PTOK, PTOK), 0) < iota((PTOK, PTOK), 1)).astype(F32)
    passed = exact(leave_p, before)
    meet = q_state.astype(F32) * enter_p[...]
    meet = jnp.where(
        iota((8, LANE), 0) < 1,
        jnp.sum(jnp.where(top, meet, 0.0), axis=0, keepdims=True),
        jnp.sum(jnp.where(top, 0.0, meet), axis=0, keepdims=True),
    )
    through = jnp.sum(meet * pdec[...], axis=1, keepdims=True)
    grad_p = live_p * (leave_p / dtp - ratep * (passed + through))
    gdtp_ref[...] = grad_p[0:2, :]

    def part_b(d):
        g = lax.rem(x + d, 4)
        if d:
            copy(b_out.at[0], b_all.at[slice_of(g)], ss_b.at[0], rs_b.at[g], s, r).wait_recv()
        b_g = b_ref[:, lanes(g)]
        wide = pl.ds(pl.multiple_of(g * ROWS, ROWS), ROWS)

        def pair(j):
            i = g * PER + j
            pulled = mm_nt(b_g, b_all[lanes(i), :])
            inter = wx[:, lanes(i)] * pulled
            xd = x_ref[:, lanes(i)].astype(F32) * inter
            gain = jnp.where(left, skip_ref[2 * i], skip_ref[2 * i + 1])
            grad = dxi[:, lanes(i)] + inter + gain * cot[:, lanes(i)].astype(F32)
            gx_ref[:, lanes(i)] = grad.astype(BF16)
            collect(i, -xd, xd)
            leave = jnp.sum(xd, axis=0, keepdims=True)
            row = iota((8, LANE), 0)
            slot = 2 * lax.rem(i, 4) + (iota((8, LANE), 1) >= 64).astype(jnp.int32)
            at8 = pl.ds(pl.multiple_of(i // 4 * 8, 8), 8)
            car[at8, :] = car[at8, :] + jnp.where(row == slot, leave, 0.0)

        each(0, PER, pair, 2)
        grad_b = mm_tn(pooled[g].astype(BF16), c_ref[:, lanes(g)]) + mm(xw[:, wide], b_all[wide, :])
        gb_ref[:, lanes(g)] = grad_b.astype(BF16)
        pltpu.make_async_copy(gx_ref.at[:, wide], gx_hbm.at[:, wide], out_sem.at[d]).start()

    def part_e(d):
        g = lax.rem(x + d, 4)
        if d:
            copy(e_out.at[0], e_all.at[slice_of(g)], ss_e.at[0], rs_e.at[g], s, r).wait_recv()
        c_g = c_ref[:, lanes(g)]
        wide = pl.ds(pl.multiple_of(g * ROWS, ROWS), ROWS)

        def pair(j):
            i = g * PER + j
            entry = e_all[lanes(i), :]
            seen = mm_nt(c_g, entry)
            z_hi, z_lo = halves(cw[:, lanes(i)].astype(F32) * seen)
            lane = iota((8, 2 * LANE), 1)
            slot = 2 * lax.rem(i, 4) + (lax.rem(lane, LANE) >= 64).astype(jnp.int32)
            pick = (iota((8, 2 * LANE), 0) == slot).astype(F32).astype(BF16)
            at8 = pl.ds(pl.multiple_of(i // 4 * 8, 8), 8)
            zs[at8, :] = zs[at8, :] + mm_nt(pick, jnp.concatenate([z_hi, z_lo], axis=1))
            prod = entry.astype(F32) * b_all[lanes(i), :].astype(F32)
            row = iota((8, LANE), 0)
            here = 2 * lax.rem(i, 4)
            one = jnp.sum(jnp.where(top, prod, 0.0), axis=0, keepdims=True) * decay[pl.ds(2 * i, 1), :]
            two = jnp.sum(jnp.where(top, 0.0, prod), axis=0, keepdims=True) * decay[pl.ds(2 * i + 1, 1), :]
            add = jnp.where(row == here, one, 0.0) + jnp.where(row == here + 1, two, 0.0)
            car[at8, :] = car[at8, :] + add

        each(0, PER, pair, 2)
        grad_c = mm(pooled[g].astype(BF16), b_ref[:, lanes(g)]) + mm(cw[:, wide], e_all[wide, :])
        gc_ref[:, lanes(g)] = grad_c.astype(BF16)

    part_b(0)
    part_b(1)

    @pl.when(z == 1)
    def _():
        z_copy().wait_recv()

        def body(h):
            rows = head_rows(h)
            state = t_in[rows, :].astype(F32)
            for k in range(4):
                e_out[k, rows, :] = state.astype(BF16)
                if k < 3:
                    state = dec_all[4 + k, pl.ds(h, 1), :] * state + l_all[k, rows, :].astype(F32)

        each(0, 16, body)
        give_back(e_out, e_all, e_copy)

    wait_from(8, q, lambda k: copy(gb_all.at[k], gb_all.at[k], ss_gb.at[0], rs_gb.at[k], s, r))
    total = gb_all[0]
    for k in range(1, 8):
        total = total + gb_all[k]
    go_all[r] = total.astype(BF16)
    each(1, 8, lambda d: gr_copy(d).start())

    part_b(3)
    part_b(2)
    wait_from(8, q, lambda k: copy(go_all.at[0], go_all.at[y * 8 + k], ss_gr.at[0], rs_gr.at[k], s, r))
    each(1, 4, lambda d: gy_copy(d).start())

    part_e(0)
    part_e(1)
    part_e(3)
    part_e(2)
    carried = jnp.sum(car[...], axis=1, keepdims=True)
    onward = (iota((TOK, TOK), 0) >= iota((TOK, TOK), 1)).astype(F32)
    grad_log = exact(zs[...], onward) + carried
    gdt_ref[...] = live * (xs[...] / dt_ref[...] - rates[...] * grad_log)

    def y_wait(k):
        block = go_all.at[pl.ds(pl.multiple_of(k * 8, 8), 8)]
        copy(block, block, ss_gy.at[0], rs_gy.at[k], s, r).wait_recv()

    each(1, 4, lambda d: y_wait(lax.rem(y + d, 4)))
    for k in range(32):
        gbp_ref[(k % 8) * 32 : (k % 8) * 32 + 32, (k // 8) * LANE : (k // 8 + 1) * LANE] = go_all[k]
    stores = [
        pltpu.make_async_copy(src, dst, out_sem.at[4 + n])
        for n, (src, dst) in enumerate(
            (
                (gxp_ref, gxp_hbm), (gbp_ref, gbp_hbm), (gdtp_ref, gdtp_hbm), (gb_ref, gb_hbm), (gc_ref, gc_hbm),
                (gdt_ref, gdt_hbm),
            )
        )
    ]
    for store in stores:
        store.start()

    each(1, 8, lambda d: p_copy(d).wait_send())
    each(1, 8, lambda d: pd_copy(d).wait_send())
    each(1, 8, lambda d: d_copy(d).wait_send())
    for make in (l_copy, b_copy, e_copy):
        each(1, 4, lambda d: make(d).wait_send())
    z_copy().wait_send()
    each(1, 8, lambda d: gb_copy(d).wait_send())
    each(1, 8, lambda d: gr_copy(d).wait_send())
    each(1, 4, lambda d: gy_copy(d).wait_send())
    each(1, 32, lambda d: g_copy(d).wait_send())

    @pl.when(z == 0)
    def _():
        each(1, 8, lambda d: fr_copy(d).wait_send())

    @pl.when((z == 0) & (y == x))
    def _():
        each(1, 4, lambda d: fy_copy(d).wait_send())

    def q_sent(k):
        @pl.when(jnp.logical_not((k == s) & (y == x)))
        def _():
            q_copy(k).wait_send()

    each(0, 8, q_sent)
    for d in range(4):
        wide = pl.ds(pl.multiple_of(lax.rem(x + d, 4) * ROWS, ROWS), ROWS)
        pltpu.make_async_copy(gx_ref.at[:, wide], gx_hbm.at[:, wide], out_sem.at[d]).wait()
    for store in stores:
        store.wait()


def hand_on(*refs):
    count = (len(refs) - 1) // 2
    moves = [pltpu.make_async_copy(refs[n], refs[count + n], refs[-1].at[n]) for n in range(count)]
    for move in moves:
        move.start()
    for move in moves:
        move.wait()


def local(
    x_prompt, dt_prompt, b_prompt, x_roll, dt_roll, b_roll, c_roll, rate, skip, grad_y, roll_len, prompt_len
):
    anywhere = pl.BlockSpec(memory_space=pl.ANY)
    smem = pl.BlockSpec(memory_space=pltpu.SMEM)
    V = pltpu.VMEM
    dma = pltpu.SemaphoreType.DMA
    wide = HEADS * 64
    ins = (x_prompt, dt_prompt, b_prompt, x_roll[0], dt_roll[0], b_roll[0], c_roll[0], grad_y[0])
    outs = (
        jax.ShapeDtypeStruct((PTOK, LANE), BF16),
        jax.ShapeDtypeStruct((PTOK, 512), BF16),
        jax.ShapeDtypeStruct((2, PTOK), F32),
        jax.ShapeDtypeStruct((TOK, wide), BF16),
        jax.ShapeDtypeStruct((TOK, 512), BF16),
        jax.ShapeDtypeStruct((TOK, 512), BF16),
        jax.ShapeDtypeStruct((HEADS, TOK), F32),
    )
    out = pl.pallas_call(
        kernel,
        name="mixer_backward",
        out_shape=outs,
        in_specs=[anywhere] * 8 + [smem] * 4,
        out_specs=(anywhere,) * 7,
        scratch_shapes=[V(value.shape, value.dtype) for value in ins + outs]
        + [
            V((HEADS, LANE), F32), V((HEADS, TOK), F32), V((HEADS, TOK), F32), V((HEADS, TOK), F32), V((HEADS, LANE), F32),
            V((TOK, wide), BF16), V((TOK, wide), BF16), V((TOK, wide), BF16), V((TOK, wide), F32),
            V((GROUPS, TOK, TOK), F32), V((GROUPS, TOK, TOK), F32), V((TOK, wide), F32),
            V((HEADS, TOK), F32), V((HEADS, TOK), F32), V((HEADS, LANE), F32),
            V((wide, LANE), BF16), V((wide, LANE), BF16), V((4, ROWS, LANE), BF16), V((4, ROWS, LANE), BF16),
            V((8, 16, LANE), F32), V((ROWS, LANE), BF16), V((ROWS, LANE), BF16),
            V((4, ROWS, LANE), BF16), V((4, ROWS, LANE), BF16), V((wide, LANE), BF16), V((wide, LANE), BF16),
            V((8, LANE, LANE), BF16), V((8, LANE), F32), V((8, 8, LANE), F32),
            V((8, LANE, LANE), BF16), V((LANE, LANE), F32), V((PTOK, LANE), BF16), V((PTOK, LANE), F32),
            V((ROWS, LANE), BF16), V((32, 32, LANE), BF16), V((32, LANE), F32), V((8, 32, LANE), F32),
            V((PTOK, LANE), F32), V((8, 32, LANE), F32), V((32, 32, LANE), BF16),
            dma((8,)), dma((10,)), dma((8,)), dma((8,)), dma((8,)), dma((8,)), dma((8,)), dma((8,)),
            dma((4,)), dma((4,)), dma((4,)), dma((4,)), dma, dma,
            dma((4,)), dma((8,)), dma((8,)), dma((4,)), dma((4,)), dma((4,)), dma((4,)), dma((32,)), dma((32,)),
            dma((8,)), dma((8,)), dma((8,)), dma((8,)), dma((8,)), dma((8,)), dma((4,)), dma((4,)),
        ],
        compiler_params=pltpu.CompilerParams(
            collective_id=0, has_side_effects=True, vmem_limit_bytes=60 * 1024 * 1024
        ),
        cost_estimate=pl.CostEstimate(flops=1_500_000_000, bytes_accessed=6_000_000, transcendentals=2_000_000),
    )(*ins, rate, skip, roll_len, prompt_len)
    out = pl.pallas_call(
        hand_on,
        name="hand_on",
        out_shape=outs,
        in_specs=[pl.BlockSpec(memory_space=pltpu.VMEM)] * 7,
        out_specs=(anywhere,) * 7,
        scratch_shapes=[dma((7,))],
    )(*out)
    gxp, gbp, gdtp, gx, gb, gc, gdt = out
    return gxp, gbp, gdtp, gx[None], gb[None], gc[None], gdt[None]


def solution(mesh):
    in_specs = (
        P("seq", "roll"), P("roll", "seq"), P("seq", None), P("roll", "seq", None), P("roll", None, "seq"),
        P("roll", "seq", None), P("roll", "seq", None), P(), P(), P("roll", "seq", None), P("roll"), P(),
    )
    out_specs = (
        P("seq", "roll"), P("seq", None), P("roll", "seq"), P("roll", "seq", None), P("roll", "seq", None),
        P("roll", "seq", None), P("roll", None, "seq"),
    )
    return jax.shard_map(local, mesh=mesh, in_specs=in_specs, out_specs=out_specs, check_vma=False)
```

time: 130 us -> 95.3 us (0.73)
  Pallas kernels: 115 us -> 92.6 us
  local copies, waits for them, and re-layouts: 12.2 us -> 0 us
    pallas_call x1 -> x2, Pallas kernels: 115 us -> 92.6 us  [the longest x1 90 us: local(): pl.pallas_call(kernel, name='mixer_backward', out_shape=outs, in_specs=[a...]
    unnamed x23 -> x0, local copies, waits for them, and re-layouts: 10.7 us -> none
    broadcast_in_dim x2 -> x0, local copies, waits for them, and re-layouts: 1.46 us -> none  [the longest x1 0.73 us: local(): skip_b = jnp.repeat(skip, 64)[None]]
where the time goes in v2:
time: 95.3 us; the launch traced here: 94.6 us
  Pallas kernels  92.6 us (97%)
  between operations  1.94 us (2%)
    pallas_call x1, Pallas kernels, local(): pl.pallas_call(kernel, name='mixer_backward', out_shape=outs, in_specs=[a...  90 us
    pallas_call x1, Pallas kernels, local(): pl.pallas_call(hand_on, name='hand_on', out_shape=outs, in_specs=[pl.Bloc...  2.59 us

profile of v2, /device:TPU:1, one launch (start us, length us, event | category | flops | bytes accessed | tf_op | source)
XLA Modules:
  0.0 94.6 jit_solution(11124623203568806644)
XLA Ops:
  1.9 90.0 %mixer_backward.1 = (bf16[256,128]{1,0:T(8,128)(2,1)}, bf16[256,512]{1,0:T(8,128)(2,1)}, f32[2,256]{1,0:T(2,128)}, bf16[128,4096]{1,0:T(8,128)(2,1)}, bf16[128,5...) custom-call(bf16[256,128]{1,0:T(8,128)(2,1)} %xp_hbm.1, f32[2,256]{1,0:T(2,128)} %dtp_hbm.1, ...), custom_call_target="tpu_custom_call" | custom-call | flops 1500000000 | bytes 6000000 | tf_op jit(solution)/shard_map/mixer_backward/pallas_call | solution.py:637
  92.0 2.6 %hand_on.1 = (bf16[256,128]{1,0:T(8,128)(2,1)}, bf16[256,512]{1,0:T(8,128)(2,1)}, f32[2,256]{1,0:T(2,128)}, bf16[128,4096]{1,0:T(8,128)(2,1)}, bf16[128,512]{1,0...) custom-call(bf16[256,128]{1,0:T(8,128)(2,1)} %get-tuple-element.21.refs_0_, ...), custom_call_target="tpu_custom_call" | custom-call | tf_op jit(solution)/shard_map/hand_on/pallas_call | solution.py:666

commit v3 on v2

--- a/solution.py
+++ b/solution.py
@@ -67,15 +67,17 @@
     gxp_ref, gbp_ref, gdtp_ref, gx_ref, gb_ref, gc_ref, gdt_ref,
     rates, cum, wrow, step, decay, cot, xw, cw, wx, cb, pooled, dxi, zs, xs, car,
     s_loc, l_loc, s_all, l_all, dec_all, t_out, t_in, e_out, b_out, e_all, b_all,
-    p_all, pdec, pdec_all, fork_all, enter_p, xw_p, wx_p,
-    back, fg_all, fg_out, q_all, gbo, gb_all, go_all,
+    p_all, pdec, pdec_all, half_out, half_in, hdec_out, hdec_in, fork_all, enter_p, xw_p, wx_p,
+    back, sib_in, fg_pieces, fg_all, fg_out, q_all, gbo, gb_all, go_all,
     in_sem, out_sem, ss_p, rs_p, ss_pd, rs_pd, ss_d, rs_d, ss_s, rs_s, ss_l, rs_l, ss_z, rs_z,
-    ss_fy, ss_fr, rs_f, ss_b, rs_b, ss_e, rs_e, ss_g, rs_g, ss_q, rs_q, ss_gb, rs_gb, ss_gr, rs_gr, ss_gy, rs_gy,
+    ss_h, rs_h, ss_fy, ss_fr, rs_f, ss_fc, rs_fc, ss_k, rs_k, ss_b, rs_b, ss_e, rs_e, ss_g, rs_g, ss_q, rs_q, ss_gb, rs_gb, ss_gr, rs_gr, ss_gy, rs_gy,
 ):
     s = lax.axis_index("seq")
     r = lax.axis_index("roll")
     z, x = s // 4, s % 4
     y, q = r // 8, r % 8
+    deep, core = q // 2, q % 2
+    sibling = r + 1 - 2 * core
 
     loads = [
         pltpu.make_async_copy(src, dst, in_sem.at[n])
@@ -134,10 +136,14 @@
         return pl.ds(pl.multiple_of(i * LANE, LANE), LANE)
 
     def p_copy(d):
-        return copy(p_all.at[s], p_all.at[s], ss_p.at[d], rs_p.at[s], lax.rem(s + d, 8), r)
+        return copy(p_all.at[x], p_all.at[x], ss_p.at[d], rs_p.at[x], z * 4 + lax.rem(x + d, 4), r)
 
     def pd_copy(d):
-        return copy(pdec, pdec_all.at[s], ss_pd.at[d], rs_pd.at[s], lax.rem(s + d, 8), r)
+        return copy(pdec, pdec_all.at[x], ss_pd.at[d], rs_pd.at[x], z * 4 + lax.rem(x + d, 4), r)
+
+    def h_copy(n):
+        out, there = ((half_out, half_in), (hdec_out, hdec_in))[n]
+        return copy(out, there, ss_h.at[n], rs_h.at[n], (1 - z) * 4 + x, r)
 
     def d_copy(d):
         to = lax.rem(s + d, 8)
@@ -152,27 +158,45 @@
         k = lax.rem(x + d, 4)
         return copy(l_loc.at[slice_of(k)], l_all.at[x], ss_l.at[d], rs_l.at[x], z * 4 + k, r)
 
-    def z_copy():
-        return copy(t_out, t_in, ss_z, rs_z, (1 - z) * 4 + x, r)
+    def z_copy(n):
+        part = pl.ds(n * (ROWS // 2), ROWS // 2)
+        return copy(t_out.at[part], t_in.at[part], ss_z.at[n], rs_z.at[n], (1 - z) * 4 + x, r)
 
     def fy_copy(d):
-        return copy(fork_all.at[q], fork_all.at[q], ss_fy.at[d], rs_f.at[q], s, lax.rem(r + 8 * d, 32))
+        mine = fork_all.at[core, deep]
+        return copy(mine, mine, ss_fy.at[d], rs_f.at[deep], s, lax.rem(r + 8 * d, 32))
 
     def fr_copy(d):
-        return copy(fork_all.at[q], fork_all.at[q], ss_fr.at[d], rs_f.at[q], s, y * 8 + lax.rem(q + d, 8))
-
-    def b_copy(d):
+        mine = fork_all.at[core, deep]
+        return copy(mine, mine, ss_fr.at[d], rs_f.at[deep], s, y * 8 + lax.rem(deep + d, 4) * 2 + core)
+
+    def fc_copy():
+        return copy(fork_all.at[core], fork_all.at[core], ss_fc, rs_fc, s, sibling)
+
+    def part_of(k, n):
+        return pl.ds(pl.multiple_of(k * ROWS + n * (ROWS // 2), ROWS // 2), ROWS // 2)
+
+    def b_copy(d, n):
         k = lax.rem(x + d, 4)
-        return copy(b_out.at[k], b_all.at[slice_of(x)], ss_b.at[d], rs_b.at[x], z * 4 + k, r)
-
-    def e_copy(d):
+        src = b_out.at[k, pl.ds(n * (ROWS // 2), ROWS // 2)]
+        return copy(src, b_all.at[part_of(x, n)], ss_b.at[2 * d + n], rs_b.at[2 * x + n], z * 4 + k, r)
+
+    def e_copy(d, n):
         k = lax.rem(x + d, 4)
-        return copy(e_out.at[k], e_all.at[slice_of(x)], ss_e.at[d], rs_e.at[x], z * 4 + k, r)
+        src = e_out.at[k, pl.ds(n * (ROWS // 2), ROWS // 2)]
+        return copy(src, e_all.at[part_of(x, n)], ss_e.at[2 * d + n], rs_e.at[2 * x + n], z * 4 + k, r)
+
+    def k_copy():
+        return copy(back.at[1 - core], sib_in, ss_k, rs_k, s, sibling)
+
+    mine = y * 4 + deep
 
     def g_copy(d):
-        t = lax.rem(r + d, 32)
-        piece = pl.multiple_of(lax.rem(t, 8) * 128 + t // 8 * 32, 32)
-        return copy(back.at[pl.ds(piece, 32)], fg_all.at[r], ss_g.at[d], rs_g.at[r], s, t)
+        t = lax.rem(mine + d, 16)
+        piece = pl.ds(pl.multiple_of(lax.rem(t, 4) * 128 + t // 4 * 32, 32), 32)
+        return copy(
+            fg_pieces.at[piece], fg_all.at[mine], ss_g.at[d], rs_g.at[mine], s, t // 4 * 8 + lax.rem(t, 4) * 2 + core
+        )
 
     def q_copy(k):
         return copy(fg_out, q_all.at[z * 4 + y], ss_q.at[k], rs_q.at[z * 4 + y], k, x * 8 + q)
@@ -213,16 +237,14 @@
 
     loads[1].wait()
     loads[2].wait()
-    for d in (2, 1, 3, 0):
+    def summarize(d):
         g = lax.rem(x + d, 4)
         c_g = c_ref[:, lanes(g)]
         each(0, PER, lambda i: s_pair(g * PER + i, c_g), 4)
-        if d == 2:
-            pl.semaphore_wait(bar, 46 - (y == x).astype(jnp.int32))
-        if d:
-            s_copy(d).start()
-        else:
-            s_all[x] = s_loc[slice_of(x), :]
+
+    summarize(2)
+    pl.semaphore_wait(bar, 46 - (y == x).astype(jnp.int32))
+    s_copy(2).start()
     each(1, 8, lambda d: d_copy(d).start())
     dec_all[s] = decay[pl.ds(pl.multiple_of(x * 16, 16), 16), :]
 
@@ -243,10 +265,16 @@
     wx_p[...] = columns(w_p[0:1, :], w_p[1:2, :], LANE, PTOK)
     xw_p[...] = (xp_ref[...].astype(F32) * wx_p[...]).astype(BF16)
     bp = bp_ref[:, lanes(y)]
-    p_all[s] = mm_tn(xw_p[...], bp).astype(BF16)
-    pdec_all[s] = pdec[...]
-    each(1, 8, lambda d: p_copy(d).start())
-    each(1, 8, lambda d: pd_copy(d).start())
+    p_all[x] = mm_tn(xw_p[...], bp).astype(BF16)
+    pdec_all[x] = pdec[...]
+    each(1, 4, lambda d: p_copy(d).start())
+    each(1, 4, lambda d: pd_copy(d).start())
+
+    for d in (1, 3):
+        summarize(d)
+        s_copy(d).start()
+    summarize(0)
+    s_all[x] = s_loc[slice_of(x), :]
 
     loads[6].wait()
     loads[7].wait()
@@ -254,6 +282,22 @@
         b_g = b_ref[:, g * LANE : (g + 1) * LANE]
         each(0, PER, lambda i: l_pair(g * PER + i, b_g), 4)
     l_all[x] = l_loc[slice_of(x), :]
+
+    wait_from(4, x, lambda k: copy(p_all.at[k], p_all.at[k], ss_p.at[0], rs_p.at[k], s, r))
+    wait_from(4, x, lambda k: copy(pdec, pdec_all.at[k], ss_pd.at[0], rs_pd.at[k], s, r))
+
+    def pdecay(ref):
+        return jnp.where(top, ref[0:1, :], ref[1:2, :])
+
+    half = p_all[0].astype(F32)
+    hdec = pdec_all[0]
+    for k in range(1, 4):
+        half = pdecay(pdec_all.at[k]) * half + p_all[k].astype(F32)
+        hdec = hdec * pdec_all[k]
+    half_out[...] = half.astype(BF16)
+    hdec_out[...] = hdec
+    h_copy(0).start()
+    h_copy(1).start()
 
     for g in range(GROUPS):
         cb[g] = mm_nt(c_ref[:, g * LANE : (g + 1) * LANE], b_ref[:, g * LANE : (g + 1) * LANE])
@@ -301,34 +345,28 @@
         xd = xf * dx
         collect(i, cf * yi - xd, xd)
 
-    each(0, 8, intra)
-
-    wait_from(8, s, lambda k: copy(p_all.at[k], p_all.at[k], ss_p.at[0], rs_p.at[k], s, r))
-    wait_from(8, s, lambda k: copy(pdec, pdec_all.at[k], ss_pd.at[0], rs_pd.at[k], s, r))
-    enter_p[...] = zero
-    fork = p_all[0].astype(F32)
-    for k in range(1, 8):
-        enter_p[...] = jnp.where(k == s, fork, enter_p[...])
-        fork = jnp.where(top, pdec_all[k, 0:1, :], pdec_all[k, 1:2, :]) * fork + p_all[k].astype(F32)
-
-    @pl.when((z == 0) & (y == x))
-    def _():
-        fork_all[q] = fork.astype(BF16)
-        each(1, 4, lambda d: fy_copy(d).start())
-        each(1, 8, lambda d: fr_copy(d).start())
+    each(0, 6, intra)
 
     each(1, 4, lambda d: s_copy(d).wait_send())
     for d in (2, 1, 3):
         l_copy(d).start()
-    each(8, 12, intra)
+
+    h_copy(0).wait_recv()
+    h_copy(1).wait_recv()
+    enter_p[...] = jnp.where(z == 1, half_in[...].astype(F32), 0.0)
+    for k in range(3):
+        moved = pdecay(pdec_all.at[k]) * enter_p[...] + p_all[k].astype(F32)
+        enter_p[...] = jnp.where(k < x, moved, enter_p[...])
+
+    @pl.when((z == 0) & (y == x))
+    def _():
+        fork_all[core, deep] = (pdecay(hdec_in) * half + half_in[...].astype(F32)).astype(BF16)
+        each(1, 4, lambda d: fy_copy(d).start())
+        each(1, 4, lambda d: fr_copy(d).start())
 
     def fork_slot(k):
-        return copy(fork_all.at[k], fork_all.at[k], ss_fr.at[0], rs_f.at[k], s, r)
-
-    @pl.when((z == 0) & (y != x))
-    def _():
-        fork_slot(q).wait_recv()
-        each(1, 8, lambda d: fr_copy(d).start())
+        slot = fork_all.at[core, k]
+        return copy(slot, slot, ss_fr.at[0], rs_f.at[k], s, r)
 
     wait_from(8, s, lambda k: copy(decay.at[pl.ds(0, 16)], dec_all.at[k], ss_d.at[0], rs_d.at[k], s, r))
     wait_from(4, x, lambda k: copy(s_all.at[k], s_all.at[k], ss_s.at[0], rs_s.at[k], s, r))
@@ -336,14 +374,14 @@
     def head_rows(h):
         return pl.ds(pl.multiple_of(h * 64, 64), 64)
 
-    def give_back(out, whole, make):
+    def give_back(out, whole, make, n):
         for d in (2, 1, 3):
-            make(d).start()
-        whole[slice_of(x), :] = out[x]
-
-    def give_pieces():
-        each(1, 32, lambda d: g_copy(d).start())
-        fg_all[r] = back[pl.ds(pl.multiple_of(q * 128 + y * 32, 32), 32), :]
+            make(d, n).start()
+        whole[part_of(x, n), :] = out[x, n * (ROWS // 2) : (n + 1) * (ROWS // 2), :]
+
+    def keep_back(h, state):
+        rows = pl.ds(pl.multiple_of(h // 4 * 128 + lax.rem(h, 2) * 64, 64), 64)
+        back[lax.rem(h // 2, 2), rows, :] = state.astype(BF16)
 
     @pl.when(z == 1)
     def _():
@@ -356,12 +394,12 @@
             t_out[rows, :] = state.astype(BF16)
             for k in range(4):
                 state = dec_all[k, pl.ds(h, 1), :] * state
-            back[rows, :] = state.astype(BF16)
-
-        each(0, 16, body)
-        z_copy().start()
-        give_pieces()
-        give_back(b_out, b_all, b_copy)
+            keep_back(h, state)
+
+        for n in range(2):
+            each(8 * n, 8 * n + 8, body, 2)
+            z_copy(n).start()
+        k_copy().start()
 
     @pl.when(z == 0)
     def _():
@@ -370,16 +408,33 @@
             state = s_all[3, rows, :].astype(F32)
             for k in (2, 1, 0):
                 state = dec_all[k, pl.ds(h, 1), :] * state + s_all[k, rows, :].astype(F32)
-            back[rows, :] = state.astype(BF16)
-
-        each(0, 16, body)
-        give_pieces()
-
-    each(12, 24, intra)
-
-    wait_from(32, r, lambda k: copy(fg_all.at[k], fg_all.at[k], ss_g.at[0], rs_g.at[k], s, r))
+            keep_back(h, state)
+
+        each(0, 16, body, 2)
+        k_copy().start()
+
+    @pl.when((z == 0) & (y != x))
+    def _():
+        fork_slot(deep).wait_recv()
+        each(1, 4, lambda d: fr_copy(d).start())
+
+    each(6, 8, intra)
+
+    k_copy().wait_recv()
+    fg_pieces[...] = (back[core].astype(F32) + sib_in[...].astype(F32)).astype(BF16)
+    each(1, 16, lambda d: g_copy(d).start())
+    fg_all[mine] = fg_pieces[pl.ds(pl.multiple_of(deep * 128 + y * 32, 32), 32), :]
+
+    @pl.when(z == 0)
+    def _():
+        wait_from(4, deep, fork_slot)
+        fc_copy().start()
+
+    each(8, 14, intra)
+
+    wait_from(16, mine, lambda k: copy(fg_all.at[k], fg_all.at[k], ss_g.at[0], rs_g.at[k], s, r))
     total = fg_all[0].astype(F32)
-    for k in range(1, 32):
+    for k in range(1, 16):
         total = total + fg_all[k].astype(F32)
     fg_out[...] = total
 
@@ -394,40 +449,50 @@
     def _():
         q_all[z * 4 + y] = total
 
-    each(24, 32, intra)
+    def leave(h):
+        rows = head_rows(h)
+        state = t_in[rows, :].astype(F32)
+        for k in (3, 2, 1, 0):
+            b_out[k, rows, :] = state.astype(BF16)
+            if k:
+                state = dec_all[k, pl.ds(h, 1), :] * state + s_all[k, rows, :].astype(F32)
+
+    def leave_half(n):
+        z_copy(n).wait_recv()
+        each(8 * n, 8 * n + 8, leave, 2)
+        give_back(b_out, b_all, b_copy, n)
+
+    @pl.when(z == 1)
+    def _():
+        for n in range(2):
+            give_back(b_out, b_all, b_copy, n)
 
     @pl.when(z == 0)
     def _():
-        z_copy().wait_recv()
-
-        def body(h):
+        leave_half(0)
+
+    @pl.when(z == 0)
+    def _():
+        wait_from(4, x, lambda k: copy(l_all.at[k], l_all.at[k], ss_l.at[0], rs_l.at[k], s, r))
+        copy(fork_all.at[0], fork_all.at[1 - core], ss_fc, rs_fc, s, r).wait_recv()
+
+        def enter(h):
             rows = head_rows(h)
-            state = t_in[rows, :].astype(F32)
-            for k in (3, 2, 1, 0):
-                b_out[k, rows, :] = state.astype(BF16)
-                if k:
-                    state = dec_all[k, pl.ds(h, 1), :] * state + s_all[k, rows, :].astype(F32)
-
-        each(0, 16, body)
-        give_back(b_out, b_all, b_copy)
-
-    wait_from(4, x, lambda k: copy(l_all.at[k], l_all.at[k], ss_l.at[0], rs_l.at[k], s, r))
-
-    @pl.when(z == 0)
-    def _():
-        wait_from(8, q, fork_slot)
-
-        def body(h):
-            rows = head_rows(h)
-            state = fork_all[h // 2, pl.ds(pl.multiple_of(lax.rem(h, 2) * 64, 64), 64), :].astype(F32)
+            first = pl.ds(pl.multiple_of(lax.rem(h, 2) * 64, 64), 64)
+            state = fork_all[lax.rem(h // 2, 2), h // 4, first, :].astype(F32)
             for k in range(4):
                 e_out[k, rows, :] = state.astype(BF16)
                 state = dec_all[k, pl.ds(h, 1), :] * state + l_all[k, rows, :].astype(F32)
             t_out[rows, :] = state.astype(BF16)
 
-        each(0, 16, body)
-        z_copy().start()
-        give_back(e_out, e_all, e_copy)
+        for n in range(2):
+            each(8 * n, 8 * n + 8, enter, 2)
+            z_copy(n).start()
+        leave_half(1)
+        for n in range(2):
+            give_back(e_out, e_all, e_copy, n)
+
+    each(14, 24, intra)
 
     def q_wait(k):
         @pl.when(jnp.logical_not((s == k // 4 * 4 + y) & (y == k % 4)))
@@ -436,8 +501,9 @@
 
     each(0, 8, q_wait)
     q_whole = jnp.concatenate([q_all[k] + q_all[4 + k] for k in range(4)], axis=0)
-    for k in range(1, 8):
-        q_whole = q_whole * jnp.where(k > s, jnp.where(top, pdec_all[k, 0:1, :], pdec_all[k, 1:2, :]), 1.0)
+    q_whole = q_whole * jnp.where(z == 0, pdecay(hdec_in), 1.0)
+    for k in range(1, 4):
+        q_whole = q_whole * jnp.where(k > x, pdecay(pdec_all.at[k]), 1.0)
     q_state = q_whole.astype(BF16)
     pulled_p = mm_nt(bp, q_state)
     dx_p = wx_p[...] * pulled_p
@@ -461,10 +527,21 @@
     grad_p = live_p * (leave_p / dtp - ratep * (passed + through))
     gdtp_ref[...] = grad_p[0:2, :]
 
+    each(24, 32, intra)
+
+    wait_from(8, q, lambda k: copy(gb_all.at[k], gb_all.at[k], ss_gb.at[0], rs_gb.at[k], s, r))
+    total = gb_all[0]
+    for k in range(1, 8):
+        total = total + gb_all[k]
+    go_all[r] = total.astype(BF16)
+    each(1, 8, lambda d: gr_copy(d).start())
+
     def part_b(d):
         g = lax.rem(x + d, 4)
         if d:
-            copy(b_out.at[0], b_all.at[slice_of(g)], ss_b.at[0], rs_b.at[g], s, r).wait_recv()
+            for n in range(2):
+                half_slice = b_all.at[part_of(g, n)]
+                copy(half_slice, half_slice, ss_b.at[0], rs_b.at[2 * g + n], s, r).wait_recv()
         b_g = b_ref[:, lanes(g)]
         wide = pl.ds(pl.multiple_of(g * ROWS, ROWS), ROWS)
 
@@ -491,7 +568,9 @@
     def part_e(d):
         g = lax.rem(x + d, 4)
         if d:
-            copy(e_out.at[0], e_all.at[slice_of(g)], ss_e.at[0], rs_e.at[g], s, r).wait_recv()
+            for n in range(2):
+                half_slice = e_all.at[part_of(g, n)]
+                copy(half_slice, half_slice, ss_e.at[0], rs_e.at[2 * g + n], s, r).wait_recv()
         c_g = c_ref[:, lanes(g)]
         wide = pl.ds(pl.multiple_of(g * ROWS, ROWS), ROWS)
 
@@ -518,13 +597,12 @@
         gc_ref[:, lanes(g)] = grad_c.astype(BF16)
 
     part_b(0)
-    part_b(1)
 
     @pl.when(z == 1)
     def _():
-        z_copy().wait_recv()
-
-        def body(h):
+        wait_from(4, x, lambda k: copy(l_all.at[k], l_all.at[k], ss_l.at[0], rs_l.at[k], s, r))
+
+        def enter(h):
             rows = head_rows(h)
             state = t_in[rows, :].astype(F32)
             for k in range(4):
@@ -532,20 +610,16 @@
                 if k < 3:
                     state = dec_all[4 + k, pl.ds(h, 1), :] * state + l_all[k, rows, :].astype(F32)
 
-        each(0, 16, body)
-        give_back(e_out, e_all, e_copy)
-
-    wait_from(8, q, lambda k: copy(gb_all.at[k], gb_all.at[k], ss_gb.at[0], rs_gb.at[k], s, r))
-    total = gb_all[0]
-    for k in range(1, 8):
-        total = total + gb_all[k]
-    go_all[r] = total.astype(BF16)
-    each(1, 8, lambda d: gr_copy(d).start())
-
+        for n in range(2):
+            z_copy(n).wait_recv()
+            each(8 * n, 8 * n + 8, enter, 2)
+            give_back(e_out, e_all, e_copy, n)
+
+    wait_from(8, q, lambda k: copy(go_all.at[0], go_all.at[y * 8 + k], ss_gr.at[0], rs_gr.at[k], s, r))
+    each(1, 4, lambda d: gy_copy(d).start())
+    part_b(1)
     part_b(3)
     part_b(2)
-    wait_from(8, q, lambda k: copy(go_all.at[0], go_all.at[y * 8 + k], ss_gr.at[0], rs_gr.at[k], s, r))
-    each(1, 4, lambda d: gy_copy(d).start())
 
     part_e(0)
     part_e(1)
@@ -575,20 +649,24 @@
     for store in stores:
         store.start()
 
-    each(1, 8, lambda d: p_copy(d).wait_send())
-    each(1, 8, lambda d: pd_copy(d).wait_send())
     each(1, 8, lambda d: d_copy(d).wait_send())
-    for make in (l_copy, b_copy, e_copy):
+    for make in (p_copy, pd_copy, l_copy):
         each(1, 4, lambda d: make(d).wait_send())
-    z_copy().wait_send()
+    for n in range(2):
+        for make in (b_copy, e_copy):
+            each(1, 4, lambda d: make(d, n).wait_send())
+        z_copy(n).wait_send()
+        h_copy(n).wait_send()
+    k_copy().wait_send()
     each(1, 8, lambda d: gb_copy(d).wait_send())
     each(1, 8, lambda d: gr_copy(d).wait_send())
     each(1, 4, lambda d: gy_copy(d).wait_send())
-    each(1, 32, lambda d: g_copy(d).wait_send())
+    each(1, 16, lambda d: g_copy(d).wait_send())
 
     @pl.when(z == 0)
     def _():
-        each(1, 8, lambda d: fr_copy(d).wait_send())
+        each(1, 4, lambda d: fr_copy(d).wait_send())
+        fc_copy().wait_send()
 
     @pl.when((z == 0) & (y == x))
     def _():
@@ -649,13 +727,16 @@
             V((wide, LANE), BF16), V((wide, LANE), BF16), V((4, ROWS, LANE), BF16), V((4, ROWS, LANE), BF16),
             V((8, 16, LANE), F32), V((ROWS, LANE), BF16), V((ROWS, LANE), BF16),
             V((4, ROWS, LANE), BF16), V((4, ROWS, LANE), BF16), V((wide, LANE), BF16), V((wide, LANE), BF16),
-            V((8, LANE, LANE), BF16), V((8, LANE), F32), V((8, 8, LANE), F32),
-            V((8, LANE, LANE), BF16), V((LANE, LANE), F32), V((PTOK, LANE), BF16), V((PTOK, LANE), F32),
-            V((ROWS, LANE), BF16), V((32, 32, LANE), BF16), V((32, LANE), F32), V((8, 32, LANE), F32),
+            V((4, LANE, LANE), BF16), V((8, LANE), F32), V((4, 8, LANE), F32),
+            V((LANE, LANE), BF16), V((LANE, LANE), BF16), V((8, LANE), F32), V((8, LANE), F32),
+            V((2, 4, LANE, LANE), BF16), V((LANE, LANE), F32), V((PTOK, LANE), BF16), V((PTOK, LANE), F32),
+            V((2, ROWS // 2, LANE), BF16), V((ROWS // 2, LANE), BF16), V((ROWS // 2, LANE), BF16),
+            V((16, 32, LANE), BF16), V((32, LANE), F32), V((8, 32, LANE), F32),
             V((PTOK, LANE), F32), V((8, 32, LANE), F32), V((32, 32, LANE), BF16),
-            dma((8,)), dma((10,)), dma((8,)), dma((8,)), dma((8,)), dma((8,)), dma((8,)), dma((8,)),
-            dma((4,)), dma((4,)), dma((4,)), dma((4,)), dma, dma,
-            dma((4,)), dma((8,)), dma((8,)), dma((4,)), dma((4,)), dma((4,)), dma((4,)), dma((32,)), dma((32,)),
+            dma((8,)), dma((10,)), dma((4,)), dma((4,)), dma((4,)), dma((4,)), dma((8,)), dma((8,)),
+            dma((4,)), dma((4,)), dma((4,)), dma((4,)), dma((2,)), dma((2,)),
+            dma((2,)), dma((2,)), dma((4,)), dma((4,)), dma((4,)), dma, dma, dma, dma,
+            dma((8,)), dma((8,)), dma((8,)), dma((8,)), dma((16,)), dma((16,)),
             dma((8,)), dma((8,)), dma((8,)), dma((8,)), dma((8,)), dma((8,)), dma((4,)), dma((4,)),
         ],
         compiler_params=pltpu.CompilerParams(

time: 95.3 us -> 81.6 us (0.86)
  Pallas kernels: 92.6 us -> 79.5 us
    pallas_call x1, Pallas kernels: 90 us -> 76.9 us  [local(): pl.pallas_call(kernel, name='mixer_backward', out_shape=outs, in_specs=[a...]
where the time goes in v3:
time: 81.6 us; the launch traced here: 81.4 us
  Pallas kernels  79.5 us (97%)
  between operations  1.94 us (2%)
    pallas_call x1, Pallas kernels, local(): pl.pallas_call(kernel, name='mixer_backward', out_shape=outs, in_specs=[a...  76.9 us
    pallas_call x1, Pallas kernels, local(): pl.pallas_call(hand_on, name='hand_on', out_shape=outs, in_specs=[pl.Bloc...  2.59 us

profile of v3, /device:TPU:1, one launch (start us, length us, event | category | flops | bytes accessed | tf_op | source)
XLA Modules:
  0.0 81.4 jit_solution(2287309210136765161)
XLA Ops:
  1.9 76.9 %mixer_backward.1 = (bf16[256,128]{1,0:T(8,128)(2,1)}, bf16[256,512]{1,0:T(8,128)(2,1)}, f32[2,256]{1,0:T(2,128)}, bf16[128,4096]{1,0:T(8,128)(2,1)}, bf16[128,5...) custom-call(bf16[256,128]{1,0:T(8,128)(2,1)} %xp_hbm.1, f32[2,256]{1,0:T(2,128)} %dtp_hbm.1, ...), custom_call_target="tpu_custom_call" | custom-call | flops 1500000000 | bytes 6000000 | tf_op jit(solution)/shard_map/mixer_backward/pallas_call | solution.py:715
  78.8 2.6 %hand_on.1 = (bf16[256,128]{1,0:T(8,128)(2,1)}, bf16[256,512]{1,0:T(8,128)(2,1)}, f32[2,256]{1,0:T(2,128)}, bf16[128,4096]{1,0:T(8,128)(2,1)}, bf16[128,512]{1,0...) custom-call(bf16[256,128]{1,0:T(8,128)(2,1)} %get-tuple-element.21.refs_0_, ...), custom_call_target="tpu_custom_call" | custom-call | tf_op jit(solution)/shard_map/hand_on/pallas_call | solution.py:747

commit v4 on v3

--- a/solution.py
+++ b/solution.py
@@ -536,12 +536,11 @@
     go_all[r] = total.astype(BF16)
     each(1, 8, lambda d: gr_copy(d).start())
 
-    def part_b(d):
+    def part_b(d, n):
         g = lax.rem(x + d, 4)
         if d:
-            for n in range(2):
-                half_slice = b_all.at[part_of(g, n)]
-                copy(half_slice, half_slice, ss_b.at[0], rs_b.at[2 * g + n], s, r).wait_recv()
+            half_slice = b_all.at[part_of(g, n)]
+            copy(half_slice, half_slice, ss_b.at[0], rs_b.at[2 * g + n], s, r).wait_recv()
         b_g = b_ref[:, lanes(g)]
         wide = pl.ds(pl.multiple_of(g * ROWS, ROWS), ROWS)
 
@@ -560,17 +559,18 @@
             at8 = pl.ds(pl.multiple_of(i // 4 * 8, 8), 8)
             car[at8, :] = car[at8, :] + jnp.where(row == slot, leave, 0.0)
 
-        each(0, PER, pair, 2)
+        each(n * PER // 2, (n + 1) * PER // 2, pair, 4)
+        if n == 0:
+            return
         grad_b = mm_tn(pooled[g].astype(BF16), c_ref[:, lanes(g)]) + mm(xw[:, wide], b_all[wide, :])
         gb_ref[:, lanes(g)] = grad_b.astype(BF16)
         pltpu.make_async_copy(gx_ref.at[:, wide], gx_hbm.at[:, wide], out_sem.at[d]).start()
 
-    def part_e(d):
+    def part_e(d, n):
         g = lax.rem(x + d, 4)
         if d:
-            for n in range(2):
-                half_slice = e_all.at[part_of(g, n)]
-                copy(half_slice, half_slice, ss_e.at[0], rs_e.at[2 * g + n], s, r).wait_recv()
+            half_slice = e_all.at[part_of(g, n)]
+            copy(half_slice, half_slice, ss_e.at[0], rs_e.at[2 * g + n], s, r).wait_recv()
         c_g = c_ref[:, lanes(g)]
         wide = pl.ds(pl.multiple_of(g * ROWS, ROWS), ROWS)
 
@@ -592,11 +592,14 @@
             add = jnp.where(row == here, one, 0.0) + jnp.where(row == here + 1, two, 0.0)
             car[at8, :] = car[at8, :] + add
 
-        each(0, PER, pair, 2)
+        each(n * PER // 2, (n + 1) * PER // 2, pair, 4)
+        if n == 0:
+            return
         grad_c = mm(pooled[g].astype(BF16), b_ref[:, lanes(g)]) + mm(cw[:, wide], e_all[wide, :])
         gc_ref[:, lanes(g)] = grad_c.astype(BF16)
 
-    part_b(0)
+    part_b(0, 0)
+    part_b(0, 1)
 
     @pl.when(z == 1)
     def _():
@@ -617,14 +620,15 @@
 
     wait_from(8, q, lambda k: copy(go_all.at[0], go_all.at[y * 8 + k], ss_gr.at[0], rs_gr.at[k], s, r))
     each(1, 4, lambda d: gy_copy(d).start())
-    part_b(1)
-    part_b(3)
-    part_b(2)
-
-    part_e(0)
-    part_e(1)
-    part_e(3)
-    part_e(2)
+    for n in range(2):
+        for d in (1, 3, 2):
+            part_b(d, n)
+
+    part_e(0, 0)
+    part_e(0, 1)
+    for n in range(2):
+        for d in (1, 3, 2):
+            part_e(d, n)
     carried = jnp.sum(car[...], axis=1, keepdims=True)
     onward = (iota((TOK, TOK), 0) >= iota((TOK, TOK), 1)).astype(F32)
     grad_log = exact(zs[...], onward) + carried

time: 81.6 us -> 77.6 us (0.951)
  Pallas kernels: 79.5 us -> 75.5 us
    pallas_call x1, Pallas kernels: 76.9 us -> 72.9 us  [local(): pl.pallas_call(kernel, name='mixer_backward', out_shape=outs, in_specs=[a...]
where the time goes in v4:
time: 77.6 us; the launch traced here: 77.4 us
  Pallas kernels  75.5 us (97%)
  between operations  1.94 us (2%)
    pallas_call x1, Pallas kernels, local(): pl.pallas_call(kernel, name='mixer_backward', out_shape=outs, in_specs=[a...  72.9 us
    pallas_call x1, Pallas kernels, local(): pl.pallas_call(hand_on, name='hand_on', out_shape=outs, in_specs=[pl.Bloc...  2.59 us

profile of v4, /device:TPU:1, one launch (start us, length us, event | category | flops | bytes accessed | tf_op | source)
XLA Modules:
  0.0 77.4 jit_solution(14174612854130792846)
XLA Ops:
  1.9 72.9 %mixer_backward.1 = (bf16[256,128]{1,0:T(8,128)(2,1)}, bf16[256,512]{1,0:T(8,128)(2,1)}, f32[2,256]{1,0:T(2,128)}, bf16[128,4096]{1,0:T(8,128)(2,1)}, bf16[128,5...) custom-call(bf16[256,128]{1,0:T(8,128)(2,1)} %xp_hbm.1, f32[2,256]{1,0:T(2,128)} %dtp_hbm.1, ...), custom_call_target="tpu_custom_call" | custom-call | flops 1500000000 | bytes 6000000 | tf_op jit(solution)/shard_map/mixer_backward/pallas_call | solution.py:719
  74.8 2.6 %hand_on.1 = (bf16[256,128]{1,0:T(8,128)(2,1)}, bf16[256,512]{1,0:T(8,128)(2,1)}, f32[2,256]{1,0:T(2,128)}, bf16[128,4096]{1,0:T(8,128)(2,1)}, bf16[128,512]{1,0...) custom-call(bf16[256,128]{1,0:T(8,128)(2,1)} %get-tuple-element.21.refs_0_, ...), custom_call_target="tpu_custom_call" | custom-call | tf_op jit(solution)/shard_map/hand_on/pallas_call | solution.py:751
